TPU v7x, 256 devices: a whole 4x4x8 slice. The times are simulated.
256 devices in a mesh: section: 4 (over x), hidden: 8 (over y, core), tok: 8 (over z).
Axes of the slice: x: 4, y: 4, z: 8, core: 2. Of those that a mesh axis runs over, the one named last changes fastest.
Arguments:
- section_inputs: bfloat16 [4, 3072, 16384], P('section', 'tok', 'hidden'), may hold values from -6 to 6
- top_adjoint: bfloat16 [3072, 16384], P('tok', 'hidden'), may hold values from -6 to 6
- right_first: bfloat16 [4, 128, 128, 128], P('section', ('hidden', 'tok')), may hold values from -0.5 to 0.5
- left_first: bfloat16 [4, 128, 128, 128], P('section', ('hidden', 'tok')), may hold values from -0.5 to 0.5
- right_second: bfloat16 [4, 128, 128, 128], P('section', ('hidden', 'tok')), may hold values from -0.5 to 0.5
- left_second: bfloat16 [4, 128, 128, 128], P('section', ('hidden', 'tok')), may hold values from -0.5 to 0.5
Outputs:
- input_adjoint: bfloat16 [4, 3072, 16384], P('section', 'tok', 'hidden')
- grad_right_first: float32 [4, 128, 128, 128], P('section', ('hidden', 'tok'))
- grad_left_first: float32 [4, 128, 128, 128], P('section', ('hidden', 'tok'))
- grad_right_second: float32 [4, 128, 128, 128], P('section', ('hidden', 'tok'))
- grad_left_second: float32 [4, 128, 128, 128], P('section', ('hidden', 'tok'))
All inputs are finite; a program needn't handle non-finite values.
Results may differ from a plain program's by a relative error of at most 0.02.
Values may be sent and summed in bfloat16 or wider, within the bound.
A program may use at most 64 MiB of HBM per device.

v0:
```python
import math

import jax
import jax.numpy as jnp
from jax import lax
from jax.sharding import PartitionSpec as P

MICRO = 3


gelu_coef = 0.7978845608028654


def passed_along(block, axis, distance):
    devices = range(lax.axis_size(axis))
    route = [(i - distance, i) for i in devices if i - distance in devices]
    return lax.ppermute(block, axis, route)


def gelu_parts(preact):
    inner_arg = gelu_coef * (preact + 0.044715 * preact * preact * preact)
    squashed = jnp.tanh(inner_arg)
    activation = 0.5 * preact * (1.0 + squashed)
    derivative = 0.5 * (1.0 + squashed) + 0.5 * preact * (1.0 - squashed * squashed) * gelu_coef * (
        1.0 + 3.0 * 0.044715 * preact * preact
    )
    return (activation, derivative)


def wide_layout(values):
    return lax.all_to_all(
        lax.all_to_all(values, "hidden", split_axis=0, concat_axis=1, tiled=True),
        "tok",
        split_axis=0,
        concat_axis=2,
        tiled=True,
    )


def narrow_layout(values):
    by_token = lax.all_to_all(values, "tok", split_axis=2, concat_axis=1, tiled=True)
    return lax.all_to_all(by_token, "hidden", split_axis=0, concat_axis=1, tiled=True)


def on_device(section_inputs, top_adjoint, right_first, left_first, right_second, left_second):
    token_count = lax.axis_size("tok")
    sections = lax.axis_size("section")
    section_id = lax.axis_index("section")
    gathered_rf, gathered_ls = (
        lax.all_gather(right_first, "tok", axis=1, tiled=True),
        lax.all_gather(left_second, "tok", axis=1, tiled=True),
    )
    weight_rf = gathered_rf[0]
    weight_ls = gathered_ls[0]
    weight_lf = left_first[0]
    weight_rs = right_second[0]
    local_count = weight_rf.shape[0]
    block_size = weight_rf.shape[1]
    wide_share = weight_lf.shape[0]
    inputs_all = section_inputs[0]
    tok_rows = inputs_all.shape[0]
    local_width = inputs_all.shape[1]
    rows = tok_rows // MICRO
    grad_scale = 1.0 / math.sqrt(tok_rows * token_count)
    zeros_edge = jnp.zeros((local_count, block_size, block_size), jnp.float32)
    zeros_wide = jnp.zeros((wide_share, block_size, block_size), jnp.float32)

    def run_tick(tick_index, loop_state):
        incoming, adjoints, sum_rf, sum_lf, sum_rs, sum_ls = loop_state
        micro_index = tick_index - (sections - 1 - section_id)
        active = jnp.logical_and(micro_index >= 0, micro_index < MICRO)
        weight_on = active.astype(jnp.float32)
        clipped = jnp.clip(micro_index, 0, MICRO - 1)
        row_start = clipped * rows
        inputs = lax.dynamic_slice_in_dim(inputs_all, row_start, rows, 0).reshape(
            rows, local_count, block_size
        )
        top_rows = lax.dynamic_slice_in_dim(top_adjoint, row_start, rows, 0)
        upstream = jnp.where(section_id == sections - 1, top_rows, incoming).reshape(
            rows, local_count, block_size
        )
        first_mid = jnp.einsum(
            "tbi,bji->jbt", inputs, weight_rf, preferred_element_type=jnp.float32
        ).astype(jnp.bfloat16)
        first_wide = wide_layout(first_mid)
        first_out = jnp.einsum(
            "jbt,jkb->tjk", first_wide, weight_lf, preferred_element_type=jnp.float32
        )
        activation, derivative = gelu_parts(first_out)
        activation = activation.astype(jnp.bfloat16)
        second_mid = jnp.einsum(
            "tbi,bji->jbt", activation, weight_rs, preferred_element_type=jnp.float32
        ).astype(jnp.bfloat16)
        second_narrow = narrow_layout(second_mid)
        term_ls = jnp.einsum(
            "tjk,jbt->jkb", upstream, second_narrow, preferred_element_type=jnp.float32
        )
        grad_mid_second = jnp.einsum(
            "tjk,jkb->bjt", upstream, weight_ls, preferred_element_type=jnp.float32
        ).astype(jnp.bfloat16)
        grad_wide = wide_layout(grad_mid_second)
        term_rs = jnp.einsum(
            "bjt,tbi->bji", grad_wide, activation, preferred_element_type=jnp.float32
        )
        grad_activation = jnp.einsum(
            "bjt,bji->tbi", grad_wide, weight_rs, preferred_element_type=jnp.float32
        )
        grad_pre = (grad_activation * derivative).astype(jnp.bfloat16)
        term_lf = jnp.einsum(
            "tjk,jbt->jkb", grad_pre, first_wide, preferred_element_type=jnp.float32
        )
        grad_mid_first = jnp.einsum(
            "tjk,jkb->bjt", grad_pre, weight_lf, preferred_element_type=jnp.float32
        ).astype(jnp.bfloat16)
        grad_narrow = narrow_layout(grad_mid_first)
        term_rf = jnp.einsum(
            "bjt,tbi->bji", grad_narrow, inputs, preferred_element_type=jnp.float32
        )
        grad_input = jnp.einsum(
            "bjt,bji->tbi", grad_narrow, weight_rf, preferred_element_type=jnp.float32
        )
        adjoint = (
            (upstream.astype(jnp.float32) + grad_input)
            .astype(jnp.bfloat16)
            .reshape(rows, local_width)
        )
        previous = lax.dynamic_slice_in_dim(adjoints, row_start, rows, 0)
        adjoints = lax.dynamic_update_slice_in_dim(
            adjoints, jnp.where(active, adjoint, previous), row_start, 0
        )
        sum_rf = sum_rf + weight_on * term_rf
        sum_ls = sum_ls + weight_on * term_ls
        sum_lf = sum_lf + weight_on * term_lf
        sum_rs = sum_rs + weight_on * term_rs
        incoming = passed_along(adjoint, "section", -1)
        return (incoming, adjoints, sum_rf, sum_lf, sum_rs, sum_ls)

    initial = (
        jnp.zeros((rows, local_width), jnp.bfloat16),
        jnp.zeros((tok_rows, local_width), jnp.bfloat16),
        zeros_edge,
        zeros_wide,
        zeros_wide,
        zeros_edge,
    )
    final_state = lax.fori_loop(0, MICRO + sections - 1, run_tick, initial)
    incoming, adjoints, sum_rf, sum_lf, sum_rs, sum_ls = final_state
    sum_rf, sum_ls = (
        lax.psum_scatter(
            sum_rf.astype(jnp.bfloat16), "tok", scatter_dimension=0, tiled=True
        ).astype(jnp.float32),
        lax.psum_scatter(
            sum_ls.astype(jnp.bfloat16), "tok", scatter_dimension=0, tiled=True
        ).astype(jnp.float32),
    )
    return (
        adjoints[None],
        (grad_scale * sum_rf)[None],
        (grad_scale * sum_lf)[None],
        (grad_scale * sum_rs)[None],
        (grad_scale * sum_ls)[None],
    )


def solution(mesh):
    in_specs = (
        P("section", "tok", "hidden"),
        P("tok", "hidden"),
        P("section", ("hidden", "tok"), None, None),
        P("section", ("hidden", "tok"), None, None),
        P("section", ("hidden", "tok"), None, None),
        P("section", ("hidden", "tok"), None, None),
    )
    out_specs = (
        P("section", "tok", "hidden"),
        P("section", ("hidden", "tok"), None, None),
        P("section", ("hidden", "tok"), None, None),
        P("section", ("hidden", "tok"), None, None),
        P("section", ("hidden", "tok"), None, None),
    )
    return jax.shard_map(
        on_device, mesh=mesh, in_specs=in_specs, out_specs=out_specs, check_vma=False
    )
```

profile of v0, /device:TPU:1, one launch (start us, length us, event | category | flops | bytes accessed | tf_op | source)
XLA Modules:
  0.0 1148.2 jit_solution(15216380863364643714)
XLA Ops:
  7.3 24.1 %all_gather.7 = bf16[1,16,128,128]{3,2,0,1:T(8,128)(2,1)S(1)} all-gather(bf16[1,2,128,128]{3,2,0,1:T(8,128)(2,1)} %bitcast.215), channel_id=1, replica_groups=mesh['section'=4,'hidden'=8,'tok'=8] {'tok'}, dimensions={1}, use_global_device_ids=true | all-gather | bytes 589824 | tf_op jit(solution)/shard_map/all_gather | solution.py:50
  31.7 19.3 %all_gather.6 = bf16[1,16,128,128]{3,2,0,1:T(8,128)(2,1)S(1)} all-gather(bf16[1,2,128,128]{3,2,0,1:T(8,128)(2,1)S(1)} %bitcast.216), channel_id=1, replica_groups=mesh['section'=4,'hidden'=8,'tok'=8] {'tok'}, dimensions={1}, use_global_device_ids=true | all-gather | bytes 589824 | tf_op jit(solution)/shard_map/all_gather | solution.py:51
  54.8 1016.1 %while.26 = (s32[]{:T(128)}, bf16[128,2048]{0,1:T(8,128)(2,1)}, bf16[384,2048]{1,0:T(8,128)(2,1)}, f32[16,128,128]{2,1,0:T(8,128)}, f32[2,128,128]{2,1,0:T(8,128...) while((s32[]{:T(128)}, bf16[128,2048]{0,1:T(8,128)(2,1)}, ...), condition=%wide.region_1.2_spmd.clone, body=%wide.region_0.1_spmd.clone.sunk | while | flops 752025600 | bytes 94634968 | solution.py:146
  57.6 17.7 %all-to-all-start.2 = ((bf16[128,16,128]{2,1,0:T(8,128)(2,1)}), bf16[128,16,128]{2,1,0:T(8,128)(2,1)S(1)}, u32[]{:S(2)}, u32[]{:S(2)}) async-start(bf16[128,16,128]{2,1,0:T(8,128)(2,1)} %copy.130), calls=%async_computation.2 | async-start | bytes 1048576 | tf_op jit(solution)/shard_map/while/body/eval_jaxpr/all_to_all | solution.py:32
  103.4 16.7 %all-to-all-done.3 = bf16[16,128,128]{2,1,0:T(8,128)(2,1)S(1)} async-done(((bf16[16,128,128]{2,1,0:T(8,128)(2,1)}), bf16[16,128,128]{2,1,0:T(8,128)(2,1)S(1)}, u32[]{:S(2)}, u32[]{:S(2)}) %all-to-all-start.3) | async-done | bytes 524320 | tf_op jit(solution)/shard_map/while/body/eval_jaxpr/all_to_all | solution.py:31
  127.0 14.5 %all-to-all-done.1 = bf16[16,128,128]{2,1,0:T(8,128)(2,1)S(1)} async-done(((bf16[16,128,128]{2,1,0:T(8,128)(2,1)}), bf16[16,128,128]{2,1,0:T(8,128)(2,1)S(1)}, u32[]{:S(2)}, u32[]{:S(2)}) %all-to-all-start.1) | async-done | bytes 524320 | tf_op jit(solution)/shard_map/while/body/eval_jaxpr/all_to_all | solution.py:31
  149.8 13.1 %all-to-all-done.6 = bf16[128,2,1024]{0,1,2:T(2,128)(2,1)S(1)} async-done(((bf16[128,2,1024]{0,1,2:T(2,128)(2,1)}), bf16[128,2,1024]{0,1,2:T(2,128)(2,1)S(1)}, u32[]{:S(2)}, u32[]{:S(2)}) %all-to-all-start.6) | async-done | bytes 524320 | tf_op jit(solution)/shard_map/while/body/eval_jaxpr/all_to_all | solution.py:41
  173.2 11.7 %all-to-all-done.4 = bf16[128,2,1024]{0,1,2:T(2,128)(2,1)S(1)} async-done(((bf16[128,2,1024]{0,1,2:T(2,128)(2,1)}), bf16[128,2,1024]{0,1,2:T(2,128)(2,1)S(1)}, u32[]{:S(2)}, u32[]{:S(2)}) %all-to-all-start.4) | async-done | bytes 524320 | tf_op jit(solution)/shard_map/while/body/eval_jaxpr/all_to_all | solution.py:41
  221.0 11.8 %collective-permute-done = bf16[128,2048]{0,1:T(8,128)(2,1)S(1)} collective-permute-done((bf16[128,2048]{0,1:T(8,128)(2,1)S(1)}, bf16[128,2048]{0,1:T(8,128)(2,1)S(1)}, u32[]{:S(2)}, u32[]{:S(2)}) %collective-permute-start) | collective-permute-done | bytes 524320 | tf_op jit(solution)/shard_map/while/body/eval_jaxpr/ppermute | solution.py:17
  269.2 17.0 %all-to-all-done.3 = bf16[16,128,128]{2,1,0:T(8,128)(2,1)S(1)} async-done(((bf16[16,128,128]{2,1,0:T(8,128)(2,1)}), bf16[16,128,128]{2,1,0:T(8,128)(2,1)S(1)}, u32[]{:S(2)}, u32[]{:S(2)}) %all-to-all-start.3) | async-done | bytes 524320 | tf_op jit(solution)/shard_map/while/body/eval_jaxpr/all_to_all | solution.py:31
  293.1 14.5 %all-to-all-done.1 = bf16[16,128,128]{2,1,0:T(8,128)(2,1)S(1)} async-done(((bf16[16,128,128]{2,1,0:T(8,128)(2,1)}), bf16[16,128,128]{2,1,0:T(8,128)(2,1)S(1)}, u32[]{:S(2)}, u32[]{:S(2)}) %all-to-all-start.1) | async-done | bytes 524320 | tf_op jit(solution)/shard_map/while/body/eval_jaxpr/all_to_all | solution.py:31
  315.9 13.0 %all-to-all-done.6 = bf16[128,2,1024]{0,1,2:T(2,128)(2,1)S(1)} async-done(((bf16[128,2,1024]{0,1,2:T(2,128)(2,1)}), bf16[128,2,1024]{0,1,2:T(2,128)(2,1)S(1)}, u32[]{:S(2)}, u32[]{:S(2)}) %all-to-all-start.6) | async-done | bytes 524320 | tf_op jit(solution)/shard_map/while/body/eval_jaxpr/all_to_all | solution.py:41
  388.5 11.8 %collective-permute-done = bf16[128,2048]{0,1:T(8,128)(2,1)S(1)} collective-permute-done((bf16[128,2048]{0,1:T(8,128)(2,1)S(1)}, bf16[128,2048]{0,1:T(8,128)(2,1)S(1)}, u32[]{:S(2)}, u32[]{:S(2)}) %collective-permute-start) | collective-permute-done | bytes 524320 | tf_op jit(solution)/shard_map/while/body/eval_jaxpr/ppermute | solution.py:17
  436.7 17.0 %all-to-all-done.3 = bf16[16,128,128]{2,1,0:T(8,128)(2,1)S(1)} async-done(((bf16[16,128,128]{2,1,0:T(8,128)(2,1)}), bf16[16,128,128]{2,1,0:T(8,128)(2,1)S(1)}, u32[]{:S(2)}, u32[]{:S(2)}) %all-to-all-start.3) | async-done | bytes 524320 | tf_op jit(solution)/shard_map/while/body/eval_jaxpr/all_to_all | solution.py:31
  460.6 14.5 %all-to-all-done.1 = bf16[16,128,128]{2,1,0:T(8,128)(2,1)S(1)} async-done(((bf16[16,128,128]{2,1,0:T(8,128)(2,1)}), bf16[16,128,128]{2,1,0:T(8,128)(2,1)S(1)}, u32[]{:S(2)}, u32[]{:S(2)}) %all-to-all-start.1) | async-done | bytes 524320 | tf_op jit(solution)/shard_map/while/body/eval_jaxpr/all_to_all | solution.py:31
  483.4 13.1 %all-to-all-done.6 = bf16[128,2,1024]{0,1,2:T(2,128)(2,1)S(1)} async-done(((bf16[128,2,1024]{0,1,2:T(2,128)(2,1)}), bf16[128,2,1024]{0,1,2:T(2,128)(2,1)S(1)}, u32[]{:S(2)}, u32[]{:S(2)}) %all-to-all-start.6) | async-done | bytes 524320 | tf_op jit(solution)/shard_map/while/body/eval_jaxpr/all_to_all | solution.py:41
  555.9 11.8 %collective-permute-done = bf16[128,2048]{0,1:T(8,128)(2,1)S(1)} collective-permute-done((bf16[128,2048]{0,1:T(8,128)(2,1)S(1)}, bf16[128,2048]{0,1:T(8,128)(2,1)S(1)}, u32[]{:S(2)}, u32[]{:S(2)}) %collective-permute-start) | collective-permute-done | bytes 524320 | tf_op jit(solution)/shard_map/while/body/eval_jaxpr/ppermute | solution.py:17
  604.1 17.0 %all-to-all-done.3 = bf16[16,128,128]{2,1,0:T(8,128)(2,1)S(1)} async-done(((bf16[16,128,128]{2,1,0:T(8,128)(2,1)}), bf16[16,128,128]{2,1,0:T(8,128)(2,1)S(1)}, u32[]{:S(2)}, u32[]{:S(2)}) %all-to-all-start.3) | async-done | bytes 524320 | tf_op jit(solution)/shard_map/while/body/eval_jaxpr/all_to_all | solution.py:31
  628.0 14.5 %all-to-all-done.1 = bf16[16,128,128]{2,1,0:T(8,128)(2,1)S(1)} async-done(((bf16[16,128,128]{2,1,0:T(8,128)(2,1)}), bf16[16,128,128]{2,1,0:T(8,128)(2,1)S(1)}, u32[]{:S(2)}, u32[]{:S(2)}) %all-to-all-start.1) | async-done | bytes 524320 | tf_op jit(solution)/shard_map/while/body/eval_jaxpr/all_to_all | solution.py:31
  650.8 13.1 %all-to-all-done.6 = bf16[128,2,1024]{0,1,2:T(2,128)(2,1)S(1)} async-done(((bf16[128,2,1024]{0,1,2:T(2,128)(2,1)}), bf16[128,2,1024]{0,1,2:T(2,128)(2,1)S(1)}, u32[]{:S(2)}, u32[]{:S(2)}) %all-to-all-start.6) | async-done | bytes 524320 | tf_op jit(solution)/shard_map/while/body/eval_jaxpr/all_to_all | solution.py:41
  723.4 11.8 %collective-permute-done = bf16[128,2048]{0,1:T(8,128)(2,1)S(1)} collective-permute-done((bf16[128,2048]{0,1:T(8,128)(2,1)S(1)}, bf16[128,2048]{0,1:T(8,128)(2,1)S(1)}, u32[]{:S(2)}, u32[]{:S(2)}) %collective-permute-start) | collective-permute-done | bytes 524320 | tf_op jit(solution)/shard_map/while/body/eval_jaxpr/ppermute | solution.py:17
  771.6 17.0 %all-to-all-done.3 = bf16[16,128,128]{2,1,0:T(8,128)(2,1)S(1)} async-done(((bf16[16,128,128]{2,1,0:T(8,128)(2,1)}), bf16[16,128,128]{2,1,0:T(8,128)(2,1)S(1)}, u32[]{:S(2)}, u32[]{:S(2)}) %all-to-all-start.3) | async-done | bytes 524320 | tf_op jit(solution)/shard_map/while/body/eval_jaxpr/all_to_all | solution.py:31
  795.5 14.5 %all-to-all-done.1 = bf16[16,128,128]{2,1,0:T(8,128)(2,1)S(1)} async-done(((bf16[16,128,128]{2,1,0:T(8,128)(2,1)}), bf16[16,128,128]{2,1,0:T(8,128)(2,1)S(1)}, u32[]{:S(2)}, u32[]{:S(2)}) %all-to-all-start.1) | async-done | bytes 524320 | tf_op jit(solution)/shard_map/while/body/eval_jaxpr/all_to_all | solution.py:31
  818.3 13.1 %all-to-all-done.6 = bf16[128,2,1024]{0,1,2:T(2,128)(2,1)S(1)} async-done(((bf16[128,2,1024]{0,1,2:T(2,128)(2,1)}), bf16[128,2,1024]{0,1,2:T(2,128)(2,1)S(1)}, u32[]{:S(2)}, u32[]{:S(2)}) %all-to-all-start.6) | async-done | bytes 524320 | tf_op jit(solution)/shard_map/while/body/eval_jaxpr/all_to_all | solution.py:41
  841.7 11.7 %all-to-all-done.4 = bf16[128,2,1024]{0,1,2:T(2,128)(2,1)S(1)} async-done(((bf16[128,2,1024]{0,1,2:T(2,128)(2,1)}), bf16[128,2,1024]{0,1,2:T(2,128)(2,1)S(1)}, u32[]{:S(2)}, u32[]{:S(2)}) %all-to-all-start.4) | async-done | bytes 524320 | tf_op jit(solution)/shard_map/while/body/eval_jaxpr/all_to_all | solution.py:41
  890.9 11.8 %collective-permute-done = bf16[128,2048]{0,1:T(8,128)(2,1)S(1)} collective-permute-done((bf16[128,2048]{0,1:T(8,128)(2,1)S(1)}, bf16[128,2048]{0,1:T(8,128)(2,1)S(1)}, u32[]{:S(2)}, u32[]{:S(2)}) %collective-permute-start) | collective-permute-done | bytes 524320 | tf_op jit(solution)/shard_map/while/body/eval_jaxpr/ppermute | solution.py:17
  939.0 17.0 %all-to-all-done.3 = bf16[16,128,128]{2,1,0:T(8,128)(2,1)S(1)} async-done(((bf16[16,128,128]{2,1,0:T(8,128)(2,1)}), bf16[16,128,128]{2,1,0:T(8,128)(2,1)S(1)}, u32[]{:S(2)}, u32[]{:S(2)}) %all-to-all-start.3) | async-done | bytes 524320 | tf_op jit(solution)/shard_map/while/body/eval_jaxpr/all_to_all | solution.py:31
  963.0 14.5 %all-to-all-done.1 = bf16[16,128,128]{2,1,0:T(8,128)(2,1)S(1)} async-done(((bf16[16,128,128]{2,1,0:T(8,128)(2,1)}), bf16[16,128,128]{2,1,0:T(8,128)(2,1)S(1)}, u32[]{:S(2)}, u32[]{:S(2)}) %all-to-all-start.1) | async-done | bytes 524320 | tf_op jit(solution)/shard_map/while/body/eval_jaxpr/all_to_all | solution.py:31
  985.7 13.1 %all-to-all-done.6 = bf16[128,2,1024]{0,1,2:T(2,128)(2,1)S(1)} async-done(((bf16[128,2,1024]{0,1,2:T(2,128)(2,1)}), bf16[128,2,1024]{0,1,2:T(2,128)(2,1)S(1)}, u32[]{:S(2)}, u32[]{:S(2)}) %all-to-all-start.6) | async-done | bytes 524320 | tf_op jit(solution)/shard_map/while/body/eval_jaxpr/all_to_all | solution.py:41
  1058.3 11.8 %collective-permute-done = bf16[128,2048]{0,1:T(8,128)(2,1)S(1)} collective-permute-done((bf16[128,2048]{0,1:T(8,128)(2,1)S(1)}, bf16[128,2048]{0,1:T(8,128)(2,1)S(1)}, u32[]{:S(2)}, u32[]{:S(2)}) %collective-permute-start) | collective-permute-done | bytes 524320 | tf_op jit(solution)/shard_map/while/body/eval_jaxpr/ppermute | solution.py:17
  1074.8 26.4 %reduce-scatter.5.cloned.1.call-done = bf16[2,128,128]{2,1,0:T(8,128)(2,1)} async-done(((bf16[16,128,128]{2,1,0:T(8,128)(2,1)}), bf16[2,128,128]{2,1,0:T(8,128)(2,1)}) %reduce-scatter.5.cloned.1.call-update) | async-done | bytes 65552 | tf_op jit(solution)/shard_map/reduce_scatter | solution.py:152
  1102.8 37.1 %reduce-scatter.3.cloned.1.call-done = bf16[2,128,128]{2,1,0:T(8,128)(2,1)} async-done(((bf16[16,128,128]{2,1,0:T(8,128)(2,1)}), bf16[2,128,128]{2,1,0:T(8,128)(2,1)}) %reduce-scatter.3.cloned.1.call-update) | async-done | bytes 65552 | tf_op jit(solution)/shard_map/reduce_scatter | solution.py:149
  (468 shorter events, 647.0 us)
Async XLA Ops:
  7.2 1094.1 %reduce-scatter.5.cloned.1.call-start = ((), (), s32[]{:S(2)}) async-start(), calls=%async_computation.11 | async-start | bytes 589824 | tf_op jit(solution)/shard_map/reduce_scatter | solution.py:152
  57.6 27.1 %all-to-all-start.2 = ((bf16[128,16,128]{2,1,0:T(8,128)(2,1)}), bf16[128,16,128]{2,1,0:T(8,128)(2,1)S(1)}, u32[]{:S(2)}, u32[]{:S(2)}) async-start(bf16[128,16,128]{2,1,0:T(8,128)(2,1)} %copy.130), calls=%async_computation.2 | async-start | bytes 1048576 | tf_op jit(solution)/shard_map/while/body/eval_jaxpr/all_to_all | solution.py:32
  98.5 21.6 %all-to-all-start.3 = ((bf16[16,128,128]{2,1,0:T(8,128)(2,1)}), bf16[16,128,128]{2,1,0:T(8,128)(2,1)S(1)}, u32[]{:S(2)}, u32[]{:S(2)}) async-start(bf16[16,128,128]{2,1,0:T(8,128)(2,1)} %bitcast.202), calls=%async_computation.3 | async-start | bytes 1048576 | tf_op jit(solution)/shard_map/while/body/eval_jaxpr/all_to_all | solution.py:31
  120.1 21.4 %all-to-all-start.1 = ((bf16[16,128,128]{2,1,0:T(8,128)(2,1)}), bf16[16,128,128]{2,1,0:T(8,128)(2,1)S(1)}, u32[]{:S(2)}, u32[]{:S(2)}) async-start(bf16[16,128,128]{2,1,0:T(8,128)(2,1)} %bitcast.171), calls=%async_computation.1 | async-start | bytes 1048576 | tf_op jit(solution)/shard_map/while/body/eval_jaxpr/all_to_all | solution.py:31
  141.5 21.4 %all-to-all-start.6 = ((bf16[128,2,1024]{0,1,2:T(2,128)(2,1)}), bf16[128,2,1024]{0,1,2:T(2,128)(2,1)S(1)}, u32[]{:S(2)}, u32[]{:S(2)}) async-start(bf16[128,2,1024]{0,1,2:T(2,128)(2,1)} %copy.140), calls=%async_computation.6 | async-start | bytes 1048576 | tf_op jit(solution)/shard_map/while/body/eval_jaxpr/all_to_all | solution.py:41
  163.6 21.4 %all-to-all-start.4 = ((bf16[128,2,1024]{0,1,2:T(2,128)(2,1)}), bf16[128,2,1024]{0,1,2:T(2,128)(2,1)S(1)}, u32[]{:S(2)}, u32[]{:S(2)}) async-start(bf16[128,2,1024]{0,1,2:T(2,128)(2,1)} %copy.133), calls=%async_computation.4 | async-start | bytes 1048576 | tf_op jit(solution)/shard_map/while/body/eval_jaxpr/all_to_all | solution.py:41
  236.4 14.7 %all-to-all-start.2 = ((bf16[128,16,128]{2,1,0:T(8,128)(2,1)}), bf16[128,16,128]{2,1,0:T(8,128)(2,1)S(1)}, u32[]{:S(2)}, u32[]{:S(2)}) async-start(bf16[128,16,128]{2,1,0:T(8,128)(2,1)} %copy.130), calls=%async_computation.2 | async-start | bytes 1048576 | tf_op jit(solution)/shard_map/while/body/eval_jaxpr/all_to_all | solution.py:32
  264.8 21.4 %all-to-all-start.3 = ((bf16[16,128,128]{2,1,0:T(8,128)(2,1)}), bf16[16,128,128]{2,1,0:T(8,128)(2,1)S(1)}, u32[]{:S(2)}, u32[]{:S(2)}) async-start(bf16[16,128,128]{2,1,0:T(8,128)(2,1)} %bitcast.202), calls=%async_computation.3 | async-start | bytes 1048576 | tf_op jit(solution)/shard_map/while/body/eval_jaxpr/all_to_all | solution.py:31
  286.2 21.4 %all-to-all-start.1 = ((bf16[16,128,128]{2,1,0:T(8,128)(2,1)}), bf16[16,128,128]{2,1,0:T(8,128)(2,1)S(1)}, u32[]{:S(2)}, u32[]{:S(2)}) async-start(bf16[16,128,128]{2,1,0:T(8,128)(2,1)} %bitcast.171), calls=%async_computation.1 | async-start | bytes 1048576 | tf_op jit(solution)/shard_map/while/body/eval_jaxpr/all_to_all | solution.py:31
  307.6 21.4 %all-to-all-start.6 = ((bf16[128,2,1024]{0,1,2:T(2,128)(2,1)}), bf16[128,2,1024]{0,1,2:T(2,128)(2,1)S(1)}, u32[]{:S(2)}, u32[]{:S(2)}) async-start(bf16[128,2,1024]{0,1,2:T(2,128)(2,1)} %copy.140), calls=%async_computation.6 | async-start | bytes 1048576 | tf_op jit(solution)/shard_map/while/body/eval_jaxpr/all_to_all | solution.py:41
  329.7 21.4 %all-to-all-start.4 = ((bf16[128,2,1024]{0,1,2:T(2,128)(2,1)}), bf16[128,2,1024]{0,1,2:T(2,128)(2,1)S(1)}, u32[]{:S(2)}, u32[]{:S(2)}) async-start(bf16[128,2,1024]{0,1,2:T(2,128)(2,1)} %copy.133), calls=%async_computation.4 | async-start | bytes 1048576 | tf_op jit(solution)/shard_map/while/body/eval_jaxpr/all_to_all | solution.py:41
  403.9 14.7 %all-to-all-start.2 = ((bf16[128,16,128]{2,1,0:T(8,128)(2,1)}), bf16[128,16,128]{2,1,0:T(8,128)(2,1)S(1)}, u32[]{:S(2)}, u32[]{:S(2)}) async-start(bf16[128,16,128]{2,1,0:T(8,128)(2,1)} %copy.130), calls=%async_computation.2 | async-start | bytes 1048576 | tf_op jit(solution)/shard_map/while/body/eval_jaxpr/all_to_all | solution.py:32
  432.3 21.4 %all-to-all-start.3 = ((bf16[16,128,128]{2,1,0:T(8,128)(2,1)}), bf16[16,128,128]{2,1,0:T(8,128)(2,1)S(1)}, u32[]{:S(2)}, u32[]{:S(2)}) async-start(bf16[16,128,128]{2,1,0:T(8,128)(2,1)} %bitcast.202), calls=%async_computation.3 | async-start | bytes 1048576 | tf_op jit(solution)/shard_map/while/body/eval_jaxpr/all_to_all | solution.py:31
  453.7 21.4 %all-to-all-start.1 = ((bf16[16,128,128]{2,1,0:T(8,128)(2,1)}), bf16[16,128,128]{2,1,0:T(8,128)(2,1)S(1)}, u32[]{:S(2)}, u32[]{:S(2)}) async-start(bf16[16,128,128]{2,1,0:T(8,128)(2,1)} %bitcast.171), calls=%async_computation.1 | async-start | bytes 1048576 | tf_op jit(solution)/shard_map/while/body/eval_jaxpr/all_to_all | solution.py:31
  475.0 21.4 %all-to-all-start.6 = ((bf16[128,2,1024]{0,1,2:T(2,128)(2,1)}), bf16[128,2,1024]{0,1,2:T(2,128)(2,1)S(1)}, u32[]{:S(2)}, u32[]{:S(2)}) async-start(bf16[128,2,1024]{0,1,2:T(2,128)(2,1)} %copy.140), calls=%async_computation.6 | async-start | bytes 1048576 | tf_op jit(solution)/shard_map/while/body/eval_jaxpr/all_to_all | solution.py:41
  497.2 21.4 %all-to-all-start.4 = ((bf16[128,2,1024]{0,1,2:T(2,128)(2,1)}), bf16[128,2,1024]{0,1,2:T(2,128)(2,1)S(1)}, u32[]{:S(2)}, u32[]{:S(2)}) async-start(bf16[128,2,1024]{0,1,2:T(2,128)(2,1)} %copy.133), calls=%async_computation.4 | async-start | bytes 1048576 | tf_op jit(solution)/shard_map/while/body/eval_jaxpr/all_to_all | solution.py:41
  571.3 14.7 %all-to-all-start.2 = ((bf16[128,16,128]{2,1,0:T(8,128)(2,1)}), bf16[128,16,128]{2,1,0:T(8,128)(2,1)S(1)}, u32[]{:S(2)}, u32[]{:S(2)}) async-start(bf16[128,16,128]{2,1,0:T(8,128)(2,1)} %copy.130), calls=%async_computation.2 | async-start | bytes 1048576 | tf_op jit(solution)/shard_map/while/body/eval_jaxpr/all_to_all | solution.py:32
  599.8 21.4 %all-to-all-start.3 = ((bf16[16,128,128]{2,1,0:T(8,128)(2,1)}), bf16[16,128,128]{2,1,0:T(8,128)(2,1)S(1)}, u32[]{:S(2)}, u32[]{:S(2)}) async-start(bf16[16,128,128]{2,1,0:T(8,128)(2,1)} %bitcast.202), calls=%async_computation.3 | async-start | bytes 1048576 | tf_op jit(solution)/shard_map/while/body/eval_jaxpr/all_to_all | solution.py:31
  621.1 21.4 %all-to-all-start.1 = ((bf16[16,128,128]{2,1,0:T(8,128)(2,1)}), bf16[16,128,128]{2,1,0:T(8,128)(2,1)S(1)}, u32[]{:S(2)}, u32[]{:S(2)}) async-start(bf16[16,128,128]{2,1,0:T(8,128)(2,1)} %bitcast.171), calls=%async_computation.1 | async-start | bytes 1048576 | tf_op jit(solution)/shard_map/while/body/eval_jaxpr/all_to_all | solution.py:31
  642.5 21.4 %all-to-all-start.6 = ((bf16[128,2,1024]{0,1,2:T(2,128)(2,1)}), bf16[128,2,1024]{0,1,2:T(2,128)(2,1)S(1)}, u32[]{:S(2)}, u32[]{:S(2)}) async-start(bf16[128,2,1024]{0,1,2:T(2,128)(2,1)} %copy.140), calls=%async_computation.6 | async-start | bytes 1048576 | tf_op jit(solution)/shard_map/while/body/eval_jaxpr/all_to_all | solution.py:41
  664.7 21.4 %all-to-all-start.4 = ((bf16[128,2,1024]{0,1,2:T(2,128)(2,1)}), bf16[128,2,1024]{0,1,2:T(2,128)(2,1)S(1)}, u32[]{:S(2)}, u32[]{:S(2)}) async-start(bf16[128,2,1024]{0,1,2:T(2,128)(2,1)} %copy.133), calls=%async_computation.4 | async-start | bytes 1048576 | tf_op jit(solution)/shard_map/while/body/eval_jaxpr/all_to_all | solution.py:41
  738.8 14.7 %all-to-all-start.2 = ((bf16[128,16,128]{2,1,0:T(8,128)(2,1)}), bf16[128,16,128]{2,1,0:T(8,128)(2,1)S(1)}, u32[]{:S(2)}, u32[]{:S(2)}) async-start(bf16[128,16,128]{2,1,0:T(8,128)(2,1)} %copy.130), calls=%async_computation.2 | async-start | bytes 1048576 | tf_op jit(solution)/shard_map/while/body/eval_jaxpr/all_to_all | solution.py:32
  767.2 21.4 %all-to-all-start.3 = ((bf16[16,128,128]{2,1,0:T(8,128)(2,1)}), bf16[16,128,128]{2,1,0:T(8,128)(2,1)S(1)}, u32[]{:S(2)}, u32[]{:S(2)}) async-start(bf16[16,128,128]{2,1,0:T(8,128)(2,1)} %bitcast.202), calls=%async_computation.3 | async-start | bytes 1048576 | tf_op jit(solution)/shard_map/while/body/eval_jaxpr/all_to_all | solution.py:31
  788.6 21.4 %all-to-all-start.1 = ((bf16[16,128,128]{2,1,0:T(8,128)(2,1)}), bf16[16,128,128]{2,1,0:T(8,128)(2,1)S(1)}, u32[]{:S(2)}, u32[]{:S(2)}) async-start(bf16[16,128,128]{2,1,0:T(8,128)(2,1)} %bitcast.171), calls=%async_computation.1 | async-start | bytes 1048576 | tf_op jit(solution)/shard_map/while/body/eval_jaxpr/all_to_all | solution.py:31
  810.0 21.4 %all-to-all-start.6 = ((bf16[128,2,1024]{0,1,2:T(2,128)(2,1)}), bf16[128,2,1024]{0,1,2:T(2,128)(2,1)S(1)}, u32[]{:S(2)}, u32[]{:S(2)}) async-start(bf16[128,2,1024]{0,1,2:T(2,128)(2,1)} %copy.140), calls=%async_computation.6 | async-start | bytes 1048576 | tf_op jit(solution)/shard_map/while/body/eval_jaxpr/all_to_all | solution.py:41
  832.1 21.4 %all-to-all-start.4 = ((bf16[128,2,1024]{0,1,2:T(2,128)(2,1)}), bf16[128,2,1024]{0,1,2:T(2,128)(2,1)S(1)}, u32[]{:S(2)}, u32[]{:S(2)}) async-start(bf16[128,2,1024]{0,1,2:T(2,128)(2,1)} %copy.133), calls=%async_computation.4 | async-start | bytes 1048576 | tf_op jit(solution)/shard_map/while/body/eval_jaxpr/all_to_all | solution.py:41
  906.3 14.7 %all-to-all-start.2 = ((bf16[128,16,128]{2,1,0:T(8,128)(2,1)}), bf16[128,16,128]{2,1,0:T(8,128)(2,1)S(1)}, u32[]{:S(2)}, u32[]{:S(2)}) async-start(bf16[128,16,128]{2,1,0:T(8,128)(2,1)} %copy.130), calls=%async_computation.2 | async-start | bytes 1048576 | tf_op jit(solution)/shard_map/while/body/eval_jaxpr/all_to_all | solution.py:32
  934.7 21.4 %all-to-all-start.3 = ((bf16[16,128,128]{2,1,0:T(8,128)(2,1)}), bf16[16,128,128]{2,1,0:T(8,128)(2,1)S(1)}, u32[]{:S(2)}, u32[]{:S(2)}) async-start(bf16[16,128,128]{2,1,0:T(8,128)(2,1)} %bitcast.202), calls=%async_computation.3 | async-start | bytes 1048576 | tf_op jit(solution)/shard_map/while/body/eval_jaxpr/all_to_all | solution.py:31
  956.1 21.4 %all-to-all-start.1 = ((bf16[16,128,128]{2,1,0:T(8,128)(2,1)}), bf16[16,128,128]{2,1,0:T(8,128)(2,1)S(1)}, u32[]{:S(2)}, u32[]{:S(2)}) async-start(bf16[16,128,128]{2,1,0:T(8,128)(2,1)} %bitcast.171), calls=%async_computation.1 | async-start | bytes 1048576 | tf_op jit(solution)/shard_map/while/body/eval_jaxpr/all_to_all | solution.py:31
  977.4 21.4 %all-to-all-start.6 = ((bf16[128,2,1024]{0,1,2:T(2,128)(2,1)}), bf16[128,2,1024]{0,1,2:T(2,128)(2,1)S(1)}, u32[]{:S(2)}, u32[]{:S(2)}) async-start(bf16[128,2,1024]{0,1,2:T(2,128)(2,1)} %copy.140), calls=%async_computation.6 | async-start | bytes 1048576 | tf_op jit(solution)/shard_map/while/body/eval_jaxpr/all_to_all | solution.py:41
  999.6 21.4 %all-to-all-start.4 = ((bf16[128,2,1024]{0,1,2:T(2,128)(2,1)}), bf16[128,2,1024]{0,1,2:T(2,128)(2,1)S(1)}, u32[]{:S(2)}, u32[]{:S(2)}) async-start(bf16[128,2,1024]{0,1,2:T(2,128)(2,1)} %copy.133), calls=%async_computation.4 | async-start | bytes 1048576 | tf_op jit(solution)/shard_map/while/body/eval_jaxpr/all_to_all | solution.py:41
  1073.1 66.7 %reduce-scatter.3.cloned.1.call-start = ((), (), s32[]{:S(2)}) async-start(), calls=%async_computation.10 | async-start | bytes 589824 | tf_op jit(solution)/shard_map/reduce_scatter | solution.py:149
  (101 other events, 751.1 us)
Sparse Core Ops, SparseCore 0:
  1073.2 27.9 reduce-scatter.4
  1103.9 35.8 reduce-scatter.2
where the time goes:
time: 1160 us; the launch traced here: 1150 us
  waiting for transfers between devices  595 us (51%)
  starting transfers between devices  213 us (18%)
  local copies, waits for them, and re-layouts  209 us (18%)
  matrix products  58.1 us (5%)
  blocking collectives  43.4 us (4%)
  between operations  14.1 us (1%)
  other arithmetic  14 us (1%)
    all_to_all x12, waiting for transfers between devices, wide_layout(): lax.all_to_all(lax.all_to_all(values, 'hidden', split_axis=0, concat_axis...  189 us
    all_to_all x12, waiting for transfers between devices, narrow_layout(): lax.all_to_all(values, 'tok', split_axis=2, concat_axis=1, tiled=True)  149 us
    all_to_all x12, waiting for transfers between devices, wide_layout(): lax.all_to_all(values, 'hidden', split_axis=0, concat_axis=1, tiled=True)  84.7 us
    all_to_all x36, local copies, waits for them, and re-layouts, narrow_layout(): lax.all_to_all(values, 'tok', split_axis=2, concat_axis=1, tiled=True)  73.9 us
    ppermute x6, waiting for transfers between devices, passed_along(): return lax.ppermute(block, axis, route)  70.6 us
    all_to_all x12, starting transfers between devices, wide_layout(): lax.all_to_all(values, 'hidden', split_axis=0, concat_axis=1, tiled=True)  69.1 us
    all_to_all x12, starting transfers between devices, narrow_layout(): lax.all_to_all(by_token, 'hidden', split_axis=0, concat_axis=1, tiled=True)  52.2 us
    all_to_all x12, starting transfers between devices, wide_layout(): lax.all_to_all(lax.all_to_all(values, 'hidden', split_axis=0, concat_axis...  42.4 us
  transfers between devices with their start and end apart: 56, of which 50 were waited for; matrix products, arithmetic and copies ran while one was open for 18% of the time, Pallas kernels for 0%

commit v1 on v0

v1 whole, which is shorter than its diff:
```python
import math

import jax
import jax.numpy as jnp
from jax import lax
from jax.sharding import PartitionSpec as P

MICRO = 3
gelu_coef = 0.7978845608028654


def passed_along(block, axis, distance):
    devices = range(lax.axis_size(axis))
    route = [(i - distance, i) for i in devices if i - distance in devices]
    return lax.ppermute(block, axis, route)


def gelu_parts(preact):
    inner_arg = gelu_coef * (preact + 0.044715 * preact * preact * preact)
    squashed = jnp.tanh(inner_arg)
    activation = 0.5 * preact * (1.0 + squashed)
    derivative = 0.5 * (1.0 + squashed) + 0.5 * preact * (1.0 - squashed * squashed) * gelu_coef * (
        1.0 + 3.0 * 0.044715 * preact * preact
    )
    return (activation, derivative)


def swap_blocks(values):
    return lax.all_to_all(values, "hidden", split_axis=0, concat_axis=1, tiled=True)


def dot(spec, a, b):
    return jnp.einsum(spec, a, b, preferred_element_type=jnp.float32)


def on_device(section_inputs, top_adjoint, right_first, left_first, right_second, left_second):
    bf = jnp.bfloat16
    sections = lax.axis_size("section")
    section_id = lax.axis_index("section")
    rf, lf, rs, ls = (
        lax.all_gather(w[0], "tok", axis=0, tiled=True)
        for w in (right_first, left_first, right_second, left_second)
    )
    local, size = rf.shape[0], rf.shape[1]
    tokens, width = top_adjoint.shape
    rows = tokens // MICRO
    scale = 1.0 / math.sqrt(tokens * lax.axis_size("tok"))
    x = section_inputs[0].reshape(tokens, local, size)
    first_mid = swap_blocks(dot("tbi,bji->jbt", x, rf).astype(bf))
    first_out = dot("jbt,jkb->jkt", first_mid, lf)
    act, der = gelu_parts(first_out)
    act = act.astype(bf)
    second_mid = swap_blocks(dot("bit,bji->jbt", act, rs).astype(bf))

    def run_tick(tick, state):
        incoming, ups_all, gm2_all, gpre_all, gm1_all, out_all = state
        micro = tick - (sections - 1 - section_id)
        active = jnp.logical_and(micro >= 0, micro < MICRO)
        start = jnp.clip(micro, 0, MICRO - 1) * rows
        top_rows = lax.dynamic_slice_in_dim(top_adjoint, start, rows, 0)
        ups_flat = jnp.where(section_id == sections - 1, top_rows, incoming)
        ups = ups_flat.reshape(rows, local, size)
        gm2 = swap_blocks(dot("tjk,jkb->bjt", ups, ls).astype(bf))
        gact = dot("bjt,bji->bit", gm2, rs)
        gpre = (gact * lax.dynamic_slice_in_dim(der, start, rows, 2)).astype(bf)
        gm1 = swap_blocks(dot("jkt,jkb->bjt", gpre, lf).astype(bf))
        ginp = dot("bjt,bji->tbi", gm1, rf)
        adjoint = (ups.astype(jnp.float32) + ginp).astype(bf).reshape(rows, width)

        def keep(whole, part, axis):
            old = lax.dynamic_slice_in_dim(whole, start, rows, axis)
            return lax.dynamic_update_slice_in_dim(whole, jnp.where(active, part, old), start, axis)

        return (
            passed_along(adjoint, "section", -1),
            keep(ups_all, ups_flat, 0),
            keep(gm2_all, gm2, 2),
            keep(gpre_all, gpre, 2),
            keep(gm1_all, gm1, 2),
            keep(out_all, adjoint, 0),
        )

    wide = jnp.zeros((local, size, tokens), bf)
    flat = jnp.zeros((tokens, width), bf)
    state = (jnp.zeros((rows, width), bf), flat, wide, wide, wide, flat)
    _, ups_all, gm2, gpre, gm1, adjoints = lax.fori_loop(0, MICRO + sections - 1, run_tick, state)
    ups = ups_all.reshape(tokens, local, size)
    g_ls = dot("tjk,jbt->jkb", ups, second_mid)
    g_rs = dot("bjt,bit->bji", gm2, act)
    g_lf = dot("jkt,jbt->jkb", gpre, first_mid)
    g_rf = dot("bjt,tbi->bji", gm1, x)
    g_rf, g_lf, g_rs, g_ls = (
        scale
        * lax.psum_scatter(g.astype(bf), "tok", scatter_dimension=0, tiled=True).astype(jnp.float32)
        for g in (g_rf, g_lf, g_rs, g_ls)
    )
    return adjoints[None], g_rf[None], g_lf[None], g_rs[None], g_ls[None]


def solution(mesh):
    act = P("section", "tok", "hidden")
    weight = P("section", ("hidden", "tok"), None, None)
    return jax.shard_map(
        on_device,
        mesh=mesh,
        in_specs=(act, P("tok", "hidden"), weight, weight, weight, weight),
        out_specs=(act, weight, weight, weight, weight),
        check_vma=False,
    )
```

time: 1160 us -> 620 us (0.53)
  waiting for transfers between devices: 595 us -> 271 us
  local copies, waits for them, and re-layouts: 209 us -> 60.4 us
  starting transfers between devices: 213 us -> 96.9 us
  blocking collectives: 43.4 us -> 86.6 us
  other arithmetic: 14 us -> 45.2 us
  matrix products: 58.1 us -> 38.4 us
    all_to_all x48 -> x14, waiting for transfers between devices: 460 us -> 108 us  [swap_blocks(): lax.all_to_all(values, 'hidden', split_axis=0, concat_axis=1, tiled=True)]
    all_to_all x48 -> x14, starting transfers between devices: 206 us -> 89 us  [swap_blocks(): lax.all_to_all(values, 'hidden', split_axis=0, concat_axis=1, tiled=True)]
    all_to_all x72 -> x26, local copies, waits for them, and re-layouts: 104 us -> 5.8 us  [swap_blocks(): lax.all_to_all(values, 'hidden', split_axis=0, concat_axis=1, tiled=True)]
    all_gather x2 -> x4, blocking collectives: 43.4 us -> 86.6 us  [on_device(): lax.all_gather(w[0], 'tok', axis=0, tiled=True)]
    reduce_scatter x2 -> x4, waiting for transfers between devices: 63.5 us -> 104 us  [on_device(): lax.psum_scatter(g.astype(bf), 'tok', scatter_dimension=0, tiled=True)]
    dynamic_update_slice x0 -> x18, other arithmetic: none -> 38.6 us  [keep(): lax.dynamic_update_slice_in_dim(whole, jnp.where(active, part, old), star...]
    while x144 -> x73, local copies, waits for them, and re-layouts: 24.8 us -> 1.19 us  [the longest x1 1.04 us: on_device(): lax.fori_loop(0, MICRO + sections - 1, run_tick, state)]
    dynamic_slice x30 -> x24, local copies, waits for them, and re-layouts: 39.5 us -> 17.3 us  [the longest x12 9.21 us: run_tick(): top_rows = lax.dynamic_slice_in_dim(top_adjoint, start, rows, 0)]
  transfers between devices with their start and end apart: 56 -> 24, of which waited for: 50 -> 22; matrix products, arithmetic and copies ran while one was open for 18% -> 10% of each run, Pallas kernels for 0% -> 0%
where the time goes in v1:
time: 620 us; the launch traced here: 613 us
  waiting for transfers between devices  271 us (44%)
  starting transfers between devices  96.9 us (16%)
  blocking collectives  86.6 us (14%)
  local copies, waits for them, and re-layouts  60.4 us (10%)
  other arithmetic  45.2 us (7%)
  matrix products  38.4 us (6%)
  between operations  13.9 us (2%)
    all_to_all x14, waiting for transfers between devices, swap_blocks(): lax.all_to_all(values, 'hidden', split_axis=0, concat_axis=1, tiled=True)  108 us
    reduce_scatter x4, waiting for transfers between devices, on_device(): lax.psum_scatter(g.astype(bf), 'tok', scatter_dimension=0, tiled=True)  104 us
    all_to_all x14, starting transfers between devices, swap_blocks(): lax.all_to_all(values, 'hidden', split_axis=0, concat_axis=1, tiled=True)  89 us
    all_gather x4, blocking collectives, on_device(): lax.all_gather(w[0], 'tok', axis=0, tiled=True)  86.6 us
    ppermute x6, waiting for transfers between devices, passed_along(): return lax.ppermute(block, axis, route)  58.5 us
    dynamic_update_slice x18, other arithmetic, keep(): lax.dynamic_update_slice_in_dim(whole, jnp.where(active, part, old), star...  38.6 us
    dot_general x31, matrix products, dot(): return jnp.einsum(spec, a, b, preferred_element_type=jnp.float32)  38.4 us
  transfers between devices with their start and end apart: 24, of which 22 were waited for; matrix products, arithmetic and copies ran while one was open for 10% of the time, Pallas kernels for 0%

profile of v1, /device:TPU:1, one launch (start us, length us, event | category | flops | bytes accessed | tf_op | source)
XLA Modules:
  0.0 612.8 jit_solution(15008810861827791230)
XLA Ops:
  7.2 24.0 %all-gather.2 = bf16[1,16,128,128]{3,2,0,1:T(8,128)(2,1)S(1)} all-gather(bf16[1,2,128,128]{3,2,0,1:T(8,128)(2,1)} %bitcast.157), channel_id=4, replica_groups=mesh['section'=4,'hidden'=8,'tok'=8] {'tok'}, dimensions={1}, use_global_device_ids=true | all-gather | bytes 589824 | tf_op jit(solution)/shard_map/all_gather | solution.py:41
  36.2 11.5 %all-to-all-start.2 = ((bf16[128,16,384]{2,1,0:T(8,128)(2,1)}), bf16[128,16,384]{2,1,0:T(8,128)(2,1)S(1)}, u32[]{:S(2)}, u32[]{:S(2)}) async-start(bf16[128,16,384]{2,1,0:T(8,128)(2,1)} %copy.85), calls=%async_computation.2 | async-start | bytes 3145728 | tf_op jit(solution)/shard_map/all_to_all | solution.py:29
  48.7 21.0 %all-gather.3 = bf16[1,16,128,128]{3,2,0,1:T(8,128)(2,1)S(1)} all-gather(bf16[1,2,128,128]{3,2,0,1:T(8,128)(2,1)S(1)} %bitcast.158), channel_id=5, replica_groups=mesh['section'=4,'hidden'=8,'tok'=8] {'tok'}, dimensions={1}, use_global_device_ids=true | all-gather | bytes 589824 | tf_op jit(solution)/shard_map/all_gather | solution.py:41
  69.8 21.5 %all-gather.1 = bf16[1,16,128,128]{3,2,0,1:T(8,128)(2,1)} all-gather(bf16[1,2,128,128]{3,2,0,1:T(8,128)(2,1)S(1)} %bitcast.159), channel_id=3, replica_groups=mesh['section'=4,'hidden'=8,'tok'=8] {'tok'}, dimensions={1}, use_global_device_ids=true | all-gather | bytes 589824 | tf_op jit(solution)/shard_map/all_gather | solution.py:41
  91.3 20.2 %all-gather = bf16[1,16,128,128]{3,2,0,1:T(8,128)(2,1)S(1)} all-gather(bf16[1,2,128,128]{3,2,0,1:T(8,128)(2,1)S(1)} %bitcast.160), channel_id=2, replica_groups=mesh['section'=4,'hidden'=8,'tok'=8] {'tok'}, dimensions={1}, use_global_device_ids=true | all-gather | bytes 589824 | tf_op jit(solution)/shard_map/all_gather | solution.py:41
  125.8 329.2 %while.25 = (s32[]{:T(128)}, bf16[128,2048]{0,1:T(8,128)(2,1)}, bf16[384,2048]{0,1:T(8,128)(2,1)}, bf16[16,128,384]{1,2,0:T(8,128)(2,1)}, bf16[16,128,384]{1,2,0...) while((s32[]{:T(128)}, bf16[128,2048]{0,1:T(8,128)(2,1)}, ...), condition=%wide.region_1.2_spmd, body=%wide.region_0.1_spmd.sunk | while | flops 271843328 | bytes 55051344 | solution.py:86
  131.2 20.5 %all-to-all-start = ((bf16[128,16,128]{2,1,0:T(8,128)(2,1)}), bf16[128,16,128]{2,1,0:T(8,128)(2,1)S(1)}, u32[]{:S(2)}, u32[]{:S(2)}) async-start(bf16[128,16,128]{2,1,0:T(8,128)(2,1)} %copy.127), calls=%async_computation | async-start | bytes 1048576 | tf_op jit(solution)/shard_map/while/body/eval_jaxpr/all_to_all | solution.py:29
  151.7 9.5 %all-to-all-done = bf16[128,16,128]{2,1,0:T(8,128)(2,1)S(1)} async-done(((bf16[128,16,128]{2,1,0:T(8,128)(2,1)}), bf16[128,16,128]{2,1,0:T(8,128)(2,1)S(1)}, u32[]{:S(2)}, u32[]{:S(2)}) %all-to-all-start) | async-done | bytes 524320 | tf_op jit(solution)/shard_map/while/body/eval_jaxpr/all_to_all | solution.py:29
  172.7 5.8 all-to-all-done.1
  183.7 9.7 %collective-permute-done = bf16[128,2048]{0,1:T(8,128)(2,1)} collective-permute-done((bf16[128,2048]{0,1:T(8,128)(2,1)S(1)}, bf16[128,2048]{0,1:T(8,128)(2,1)}, u32[]{:S(2)}, u32[]{:S(2)}) %collective-permute-start) | collective-permute-done | bytes 524320 | tf_op jit(solution)/shard_map/while/body/eval_jaxpr/ppermute | solution.py:15
  198.8 5.2 all-to-all-start
  204.0 9.5 %all-to-all-done = bf16[128,16,128]{2,1,0:T(8,128)(2,1)S(1)} async-done(((bf16[128,16,128]{2,1,0:T(8,128)(2,1)}), bf16[128,16,128]{2,1,0:T(8,128)(2,1)S(1)}, u32[]{:S(2)}, u32[]{:S(2)}) %all-to-all-start) | async-done | bytes 524320 | tf_op jit(solution)/shard_map/while/body/eval_jaxpr/all_to_all | solution.py:29
  225.0 5.8 all-to-all-done.1
  236.0 9.7 %collective-permute-done = bf16[128,2048]{0,1:T(8,128)(2,1)} collective-permute-done((bf16[128,2048]{0,1:T(8,128)(2,1)S(1)}, bf16[128,2048]{0,1:T(8,128)(2,1)}, u32[]{:S(2)}, u32[]{:S(2)}) %collective-permute-start) | collective-permute-done | bytes 524320 | tf_op jit(solution)/shard_map/while/body/eval_jaxpr/ppermute | solution.py:15
  256.3 9.5 %all-to-all-done = bf16[128,16,128]{2,1,0:T(8,128)(2,1)S(1)} async-done(((bf16[128,16,128]{2,1,0:T(8,128)(2,1)}), bf16[128,16,128]{2,1,0:T(8,128)(2,1)S(1)}, u32[]{:S(2)}, u32[]{:S(2)}) %all-to-all-start) | async-done | bytes 524320 | tf_op jit(solution)/shard_map/while/body/eval_jaxpr/all_to_all | solution.py:29
  277.3 5.8 all-to-all-done.1
  288.3 9.7 %collective-permute-done = bf16[128,2048]{0,1:T(8,128)(2,1)} collective-permute-done((bf16[128,2048]{0,1:T(8,128)(2,1)S(1)}, bf16[128,2048]{0,1:T(8,128)(2,1)}, u32[]{:S(2)}, u32[]{:S(2)}) %collective-permute-start) | collective-permute-done | bytes 524320 | tf_op jit(solution)/shard_map/while/body/eval_jaxpr/ppermute | solution.py:15
  308.6 9.5 %all-to-all-done = bf16[128,16,128]{2,1,0:T(8,128)(2,1)S(1)} async-done(((bf16[128,16,128]{2,1,0:T(8,128)(2,1)}), bf16[128,16,128]{2,1,0:T(8,128)(2,1)S(1)}, u32[]{:S(2)}, u32[]{:S(2)}) %all-to-all-start) | async-done | bytes 524320 | tf_op jit(solution)/shard_map/while/body/eval_jaxpr/all_to_all | solution.py:29
  329.7 5.8 all-to-all-done.1
  340.6 9.7 %collective-permute-done = bf16[128,2048]{0,1:T(8,128)(2,1)} collective-permute-done((bf16[128,2048]{0,1:T(8,128)(2,1)S(1)}, bf16[128,2048]{0,1:T(8,128)(2,1)}, u32[]{:S(2)}, u32[]{:S(2)}) %collective-permute-start) | collective-permute-done | bytes 524320 | tf_op jit(solution)/shard_map/while/body/eval_jaxpr/ppermute | solution.py:15
  355.8 5.2 all-to-all-start
  361.0 9.5 %all-to-all-done = bf16[128,16,128]{2,1,0:T(8,128)(2,1)S(1)} async-done(((bf16[128,16,128]{2,1,0:T(8,128)(2,1)}), bf16[128,16,128]{2,1,0:T(8,128)(2,1)S(1)}, u32[]{:S(2)}, u32[]{:S(2)}) %all-to-all-start) | async-done | bytes 524320 | tf_op jit(solution)/shard_map/while/body/eval_jaxpr/all_to_all | solution.py:29
  382.0 5.8 all-to-all-done.1
  393.0 9.8 %collective-permute-done = bf16[128,2048]{0,1:T(8,128)(2,1)} collective-permute-done((bf16[128,2048]{0,1:T(8,128)(2,1)S(1)}, bf16[128,2048]{0,1:T(8,128)(2,1)}, u32[]{:S(2)}, u32[]{:S(2)}) %collective-permute-start) | collective-permute-done | bytes 524320 | tf_op jit(solution)/shard_map/while/body/eval_jaxpr/ppermute | solution.py:15
  413.3 9.5 %all-to-all-done = bf16[128,16,128]{2,1,0:T(8,128)(2,1)S(1)} async-done(((bf16[128,16,128]{2,1,0:T(8,128)(2,1)}), bf16[128,16,128]{2,1,0:T(8,128)(2,1)S(1)}, u32[]{:S(2)}, u32[]{:S(2)}) %all-to-all-start) | async-done | bytes 524320 | tf_op jit(solution)/shard_map/while/body/eval_jaxpr/all_to_all | solution.py:29
  434.3 5.8 all-to-all-done.1
  445.3 9.7 %collective-permute-done = bf16[128,2048]{0,1:T(8,128)(2,1)} collective-permute-done((bf16[128,2048]{0,1:T(8,128)(2,1)S(1)}, bf16[128,2048]{0,1:T(8,128)(2,1)}, u32[]{:S(2)}, u32[]{:S(2)}) %collective-permute-start) | collective-permute-done | bytes 524320 | tf_op jit(solution)/shard_map/while/body/eval_jaxpr/ppermute | solution.py:15
  466.8 5.6 all-to-all-start.3
  476.7 16.4 %all-to-all-done.3 = bf16[128,16,384]{2,1,0:T(8,128)(2,1)S(1)} async-done(((bf16[128,16,384]{2,1,0:T(8,128)(2,1)}), bf16[128,16,384]{2,1,0:T(8,128)(2,1)S(1)}, u32[]{:S(2)}, u32[]{:S(2)}) %all-to-all-start.3) | async-done | bytes 1572896 | tf_op jit(solution)/shard_map/all_to_all | solution.py:29
  497.7 30.1 %reduce-scatter.5.cloned.1.call-done = bf16[2,128,128]{2,1,0:T(8,128)(2,1)} async-done(((bf16[16,128,128]{2,1,0:T(8,128)(2,1)}), bf16[2,128,128]{2,1,0:T(8,128)(2,1)}) %reduce-scatter.5.cloned.1.call-update) | async-done | bytes 65552 | tf_op jit(solution)/shard_map/reduce_scatter | solution.py:94
  529.3 36.9 %reduce-scatter.9.cloned.1.call-done = bf16[2,128,128]{2,1,0:T(8,128)(2,1)} async-done(((bf16[16,128,128]{2,1,0:T(8,128)(2,1)}), bf16[2,128,128]{2,1,0:T(8,128)(2,1)}) %reduce-scatter.9.cloned.1.call-update) | async-done | bytes 65552 | tf_op jit(solution)/shard_map/reduce_scatter | solution.py:94
  567.8 37.0 %reduce-scatter.11.cloned.1.call-done = bf16[2,128,128]{2,1,0:T(8,128)(2,1)} async-done(((bf16[16,128,128]{2,1,0:T(8,128)(2,1)}), bf16[2,128,128]{2,1,0:T(8,128)(2,1)}) %reduce-scatter.11.cloned.1.call-update) | async-done | bytes 65552 | tf_op jit(solution)/shard_map/reduce_scatter | solution.py:94
  (262 shorter events, 193.0 us)
Async XLA Ops:
  36.2 75.3 %all-to-all-start.2 = ((bf16[128,16,384]{2,1,0:T(8,128)(2,1)}), bf16[128,16,384]{2,1,0:T(8,128)(2,1)S(1)}, u32[]{:S(2)}, u32[]{:S(2)}) async-start(bf16[128,16,384]{2,1,0:T(8,128)(2,1)} %copy.85), calls=%async_computation.2 | async-start | bytes 3145728 | tf_op jit(solution)/shard_map/all_to_all | solution.py:29
  47.6 22.1 %copy-start.15 = (bf16[1,2,128,128]{3,2,1,0:T(8,128)(2,1)S(1)}, bf16[1,2,128,128]{3,2,1,0:T(8,128)(2,1)}, u32[]{:S(2)}) copy-start(bf16[1,2,128,128]{3,2,1,0:T(8,128)(2,1)} %param.12) | copy-start | bytes 196612
  47.6 43.6 %copy-start.16 = (bf16[1,2,128,128]{3,2,1,0:T(8,128)(2,1)S(1)}, bf16[1,2,128,128]{3,2,1,0:T(8,128)(2,1)}, u32[]{:S(2)}) copy-start(bf16[1,2,128,128]{3,2,1,0:T(8,128)(2,1)} %param.13) | copy-start | bytes 196612
  47.7 448.6 %reduce-scatter.7.cloned.1.call-start = ((), (), s32[]{:S(2)}) async-start(), calls=%async_computation.9 | async-start | bytes 589824 | tf_op jit(solution)/shard_map/reduce_scatter | solution.py:94
  69.8 44.5 %copy-start.4 = (bf16[1,16,128,128]{3,2,0,1:T(8,128)(2,1)}, bf16[1,16,128,128]{3,2,0,1:T(8,128)(2,1)S(1)}, u32[]{:S(2)}) copy-start(bf16[1,16,128,128]{3,2,0,1:T(8,128)(2,1)S(1)} %all-gather.3) | copy-start | bytes 1572868
  131.2 30.0 %all-to-all-start = ((bf16[128,16,128]{2,1,0:T(8,128)(2,1)}), bf16[128,16,128]{2,1,0:T(8,128)(2,1)S(1)}, u32[]{:S(2)}, u32[]{:S(2)}) async-start(bf16[128,16,128]{2,1,0:T(8,128)(2,1)} %copy.127), calls=%async_computation | async-start | bytes 1048576 | tf_op jit(solution)/shard_map/while/body/eval_jaxpr/all_to_all | solution.py:29
  164.7 13.8 %all-to-all-start.1 = ((bf16[128,16,128]{2,1,0:T(8,128)(2,1)}), bf16[128,16,128]{2,1,0:T(8,128)(2,1)S(1)}, u32[]{:S(2)}, u32[]{:S(2)}) async-start(bf16[128,16,128]{2,1,0:T(8,128)(2,1)} %copy.129), calls=%async_computation.1 | async-start | bytes 1048576 | tf_op jit(solution)/shard_map/while/body/eval_jaxpr/all_to_all | solution.py:29
  178.8 14.6 %collective-permute-start = (bf16[128,2048]{0,1:T(8,128)(2,1)S(1)}, bf16[128,2048]{0,1:T(8,128)(2,1)}, u32[]{:S(2)}, u32[]{:S(2)}) collective-permute-start(bf16[128,2048]{0,1:T(8,128)(2,1)S(1)} %bitcast.141), channel_id=1, source_target_pairs={{64,0},{128,64},{192,128},{65,1},{129,65},{193,129},{66,2},{130,66... | collective-permute-start | bytes 1572872 | tf_op jit(solution)/shard_map/while/body/eval_jaxpr/ppermute | solution.py:15
  180.7 12.7 %copy-start.2 = (bf16[16,128,384]{1,2,0:T(8,128)(2,1)S(1)}, bf16[16,128,384]{1,2,0:T(8,128)(2,1)}, u32[]{:S(2)}) copy-start(bf16[16,128,384]{1,2,0:T(8,128)(2,1)} %copy-done.1) | copy-start | bytes 4718596 | tf_op jit(solution)/shard_map/while
  198.8 14.7 %all-to-all-start = ((bf16[128,16,128]{2,1,0:T(8,128)(2,1)}), bf16[128,16,128]{2,1,0:T(8,128)(2,1)S(1)}, u32[]{:S(2)}, u32[]{:S(2)}) async-start(bf16[128,16,128]{2,1,0:T(8,128)(2,1)} %copy.127), calls=%async_computation | async-start | bytes 1048576 | tf_op jit(solution)/shard_map/while/body/eval_jaxpr/all_to_all | solution.py:29
  217.0 13.8 %all-to-all-start.1 = ((bf16[128,16,128]{2,1,0:T(8,128)(2,1)}), bf16[128,16,128]{2,1,0:T(8,128)(2,1)S(1)}, u32[]{:S(2)}, u32[]{:S(2)}) async-start(bf16[128,16,128]{2,1,0:T(8,128)(2,1)} %copy.129), calls=%async_computation.1 | async-start | bytes 1048576 | tf_op jit(solution)/shard_map/while/body/eval_jaxpr/all_to_all | solution.py:29
  231.2 14.6 %collective-permute-start = (bf16[128,2048]{0,1:T(8,128)(2,1)S(1)}, bf16[128,2048]{0,1:T(8,128)(2,1)}, u32[]{:S(2)}, u32[]{:S(2)}) collective-permute-start(bf16[128,2048]{0,1:T(8,128)(2,1)S(1)} %bitcast.141), channel_id=1, source_target_pairs={{64,0},{128,64},{192,128},{65,1},{129,65},{193,129},{66,2},{130,66... | collective-permute-start | bytes 1572872 | tf_op jit(solution)/shard_map/while/body/eval_jaxpr/ppermute | solution.py:15
  233.1 12.7 %copy-start.2 = (bf16[16,128,384]{1,2,0:T(8,128)(2,1)S(1)}, bf16[16,128,384]{1,2,0:T(8,128)(2,1)}, u32[]{:S(2)}) copy-start(bf16[16,128,384]{1,2,0:T(8,128)(2,1)} %copy-done.1) | copy-start | bytes 4718596 | tf_op jit(solution)/shard_map/while
  251.1 14.7 %all-to-all-start = ((bf16[128,16,128]{2,1,0:T(8,128)(2,1)}), bf16[128,16,128]{2,1,0:T(8,128)(2,1)S(1)}, u32[]{:S(2)}, u32[]{:S(2)}) async-start(bf16[128,16,128]{2,1,0:T(8,128)(2,1)} %copy.127), calls=%async_computation | async-start | bytes 1048576 | tf_op jit(solution)/shard_map/while/body/eval_jaxpr/all_to_all | solution.py:29
  269.3 13.8 %all-to-all-start.1 = ((bf16[128,16,128]{2,1,0:T(8,128)(2,1)}), bf16[128,16,128]{2,1,0:T(8,128)(2,1)S(1)}, u32[]{:S(2)}, u32[]{:S(2)}) async-start(bf16[128,16,128]{2,1,0:T(8,128)(2,1)} %copy.129), calls=%async_computation.1 | async-start | bytes 1048576 | tf_op jit(solution)/shard_map/while/body/eval_jaxpr/all_to_all | solution.py:29
  283.5 14.6 %collective-permute-start = (bf16[128,2048]{0,1:T(8,128)(2,1)S(1)}, bf16[128,2048]{0,1:T(8,128)(2,1)}, u32[]{:S(2)}, u32[]{:S(2)}) collective-permute-start(bf16[128,2048]{0,1:T(8,128)(2,1)S(1)} %bitcast.141), channel_id=1, source_target_pairs={{64,0},{128,64},{192,128},{65,1},{129,65},{193,129},{66,2},{130,66... | collective-permute-start | bytes 1572872 | tf_op jit(solution)/shard_map/while/body/eval_jaxpr/ppermute | solution.py:15
  285.4 12.7 %copy-start.2 = (bf16[16,128,384]{1,2,0:T(8,128)(2,1)S(1)}, bf16[16,128,384]{1,2,0:T(8,128)(2,1)}, u32[]{:S(2)}) copy-start(bf16[16,128,384]{1,2,0:T(8,128)(2,1)} %copy-done.1) | copy-start | bytes 4718596 | tf_op jit(solution)/shard_map/while
  303.4 14.7 %all-to-all-start = ((bf16[128,16,128]{2,1,0:T(8,128)(2,1)}), bf16[128,16,128]{2,1,0:T(8,128)(2,1)S(1)}, u32[]{:S(2)}, u32[]{:S(2)}) async-start(bf16[128,16,128]{2,1,0:T(8,128)(2,1)} %copy.127), calls=%async_computation | async-start | bytes 1048576 | tf_op jit(solution)/shard_map/while/body/eval_jaxpr/all_to_all | solution.py:29
  321.7 13.8 %all-to-all-start.1 = ((bf16[128,16,128]{2,1,0:T(8,128)(2,1)}), bf16[128,16,128]{2,1,0:T(8,128)(2,1)S(1)}, u32[]{:S(2)}, u32[]{:S(2)}) async-start(bf16[128,16,128]{2,1,0:T(8,128)(2,1)} %copy.129), calls=%async_computation.1 | async-start | bytes 1048576 | tf_op jit(solution)/shard_map/while/body/eval_jaxpr/all_to_all | solution.py:29
  335.8 14.6 %collective-permute-start = (bf16[128,2048]{0,1:T(8,128)(2,1)S(1)}, bf16[128,2048]{0,1:T(8,128)(2,1)}, u32[]{:S(2)}, u32[]{:S(2)}) collective-permute-start(bf16[128,2048]{0,1:T(8,128)(2,1)S(1)} %bitcast.141), channel_id=1, source_target_pairs={{64,0},{128,64},{192,128},{65,1},{129,65},{193,129},{66,2},{130,66... | collective-permute-start | bytes 1572872 | tf_op jit(solution)/shard_map/while/body/eval_jaxpr/ppermute | solution.py:15
  337.7 12.7 %copy-start.2 = (bf16[16,128,384]{1,2,0:T(8,128)(2,1)S(1)}, bf16[16,128,384]{1,2,0:T(8,128)(2,1)}, u32[]{:S(2)}) copy-start(bf16[16,128,384]{1,2,0:T(8,128)(2,1)} %copy-done.1) | copy-start | bytes 4718596 | tf_op jit(solution)/shard_map/while
  355.8 14.7 %all-to-all-start = ((bf16[128,16,128]{2,1,0:T(8,128)(2,1)}), bf16[128,16,128]{2,1,0:T(8,128)(2,1)S(1)}, u32[]{:S(2)}, u32[]{:S(2)}) async-start(bf16[128,16,128]{2,1,0:T(8,128)(2,1)} %copy.127), calls=%async_computation | async-start | bytes 1048576 | tf_op jit(solution)/shard_map/while/body/eval_jaxpr/all_to_all | solution.py:29
  374.0 13.8 %all-to-all-start.1 = ((bf16[128,16,128]{2,1,0:T(8,128)(2,1)}), bf16[128,16,128]{2,1,0:T(8,128)(2,1)S(1)}, u32[]{:S(2)}, u32[]{:S(2)}) async-start(bf16[128,16,128]{2,1,0:T(8,128)(2,1)} %copy.129), calls=%async_computation.1 | async-start | bytes 1048576 | tf_op jit(solution)/shard_map/while/body/eval_jaxpr/all_to_all | solution.py:29
  388.2 14.6 %collective-permute-start = (bf16[128,2048]{0,1:T(8,128)(2,1)S(1)}, bf16[128,2048]{0,1:T(8,128)(2,1)}, u32[]{:S(2)}, u32[]{:S(2)}) collective-permute-start(bf16[128,2048]{0,1:T(8,128)(2,1)S(1)} %bitcast.141), channel_id=1, source_target_pairs={{64,0},{128,64},{192,128},{65,1},{129,65},{193,129},{66,2},{130,66... | collective-permute-start | bytes 1572872 | tf_op jit(solution)/shard_map/while/body/eval_jaxpr/ppermute | solution.py:15
  390.1 12.7 %copy-start.2 = (bf16[16,128,384]{1,2,0:T(8,128)(2,1)S(1)}, bf16[16,128,384]{1,2,0:T(8,128)(2,1)}, u32[]{:S(2)}) copy-start(bf16[16,128,384]{1,2,0:T(8,128)(2,1)} %copy-done.1) | copy-start | bytes 4718596 | tf_op jit(solution)/shard_map/while
  408.1 14.7 %all-to-all-start = ((bf16[128,16,128]{2,1,0:T(8,128)(2,1)}), bf16[128,16,128]{2,1,0:T(8,128)(2,1)S(1)}, u32[]{:S(2)}, u32[]{:S(2)}) async-start(bf16[128,16,128]{2,1,0:T(8,128)(2,1)} %copy.127), calls=%async_computation | async-start | bytes 1048576 | tf_op jit(solution)/shard_map/while/body/eval_jaxpr/all_to_all | solution.py:29
  426.3 13.8 %all-to-all-start.1 = ((bf16[128,16,128]{2,1,0:T(8,128)(2,1)}), bf16[128,16,128]{2,1,0:T(8,128)(2,1)S(1)}, u32[]{:S(2)}, u32[]{:S(2)}) async-start(bf16[128,16,128]{2,1,0:T(8,128)(2,1)} %copy.129), calls=%async_computation.1 | async-start | bytes 1048576 | tf_op jit(solution)/shard_map/while/body/eval_jaxpr/all_to_all | solution.py:29
  440.5 14.6 %collective-permute-start = (bf16[128,2048]{0,1:T(8,128)(2,1)S(1)}, bf16[128,2048]{0,1:T(8,128)(2,1)}, u32[]{:S(2)}, u32[]{:S(2)}) collective-permute-start(bf16[128,2048]{0,1:T(8,128)(2,1)S(1)} %bitcast.141), channel_id=1, source_target_pairs={{64,0},{128,64},{192,128},{65,1},{129,65},{193,129},{66,2},{130,66... | collective-permute-start | bytes 1572872 | tf_op jit(solution)/shard_map/while/body/eval_jaxpr/ppermute | solution.py:15
  458.2 69.6 %reduce-scatter.5.cloned.1.call-start = ((), (), s32[]{:S(2)}) async-start(), calls=%async_computation.8 | async-start | bytes 589824 | tf_op jit(solution)/shard_map/reduce_scatter | solution.py:94
  466.8 26.3 %all-to-all-start.3 = ((bf16[128,16,384]{2,1,0:T(8,128)(2,1)}), bf16[128,16,384]{2,1,0:T(8,128)(2,1)S(1)}, u32[]{:S(2)}, u32[]{:S(2)}) async-start(bf16[128,16,384]{2,1,0:T(8,128)(2,1)} %copy.97), calls=%async_computation.6 | async-start | bytes 3145728 | tf_op jit(solution)/shard_map/all_to_all | solution.py:29
  472.4 93.9 %reduce-scatter.9.cloned.1.call-start = ((), (), s32[]{:S(2)}) async-start(), calls=%async_computation.10 | async-start | bytes 589824 | tf_op jit(solution)/shard_map/reduce_scatter | solution.py:94
  476.7 128.1 %reduce-scatter.11.cloned.1.call-start = ((), (), s32[]{:S(2)}) async-start(), calls=%async_computation.11 | async-start | bytes 589824 | tf_op jit(solution)/shard_map/reduce_scatter | solution.py:94
  (39 other events, 208.6 us)
Sparse Core Ops, SparseCore 0:
  458.3 31.0 reduce-scatter.6
  492.0 35.7 reduce-scatter.4
  530.4 35.8 reduce-scatter.8
  568.8 35.9 reduce-scatter.10

commit v2 on v1

v2 whole, which is shorter than its diff:
```python
import functools
import math

import jax
import jax.numpy as jnp
from jax import lax
from jax.experimental import pallas as pl
from jax.experimental.pallas import tpu as pltpu
from jax.sharding import PartitionSpec as P

MESH = pl.DeviceIdType.MESH
BF, F32 = jnp.bfloat16, jnp.float32
BLK = 128
MIC = 128
GRP = 4
COEF = 0.7978845608028654
FM, SM, GM2, GM1 = range(4)
RF, LF, RS, LS = range(4)


def gelu_parts(v):
    squashed = jnp.tanh(COEF * (v + 0.044715 * v * v * v))
    activation = 0.5 * v * (1.0 + squashed)
    derivative = 0.5 * (1.0 + squashed) + 0.5 * v * (1.0 - squashed * squashed) * COEF * (
        1.0 + 3.0 * 0.044715 * v * v
    )
    return activation, derivative


def nn(a, b):
    return lax.dot_general(a, b, (((1,), (0,)), ((), ())), preferred_element_type=F32)


def nt(a, b):
    return lax.dot_general(a, b, (((1,), (1,)), ((), ())), preferred_element_type=F32)


def tn(a, b):
    return lax.dot_general(a, b, (((0,), (0,)), ((), ())), preferred_element_type=F32)


def lanes(b, count=1):
    return pl.ds(pl.multiple_of(b * BLK, BLK), count * BLK)


def kernel(
    S, H, Z, scale,
    x, top, rf, lf, rs, ls,
    adj, o_rf, o_lf, o_rs, o_ls,
    ups, send, recv, act, der, gpre, stage, weights, turned, sums, part_send, part_recv,
    top_sem, w_send, w_recv, a_send, a_recv, p_send, p_recv, r_send, r_recv,
):
    sec, h, z = (lax.axis_index(name) for name in ("section", "hidden", "tok"))
    is_last, is_first = sec == S - 1, sec == 0
    below, above = lax.rem(sec + S - 1, S), lax.rem(sec + 1, S)
    M = x.shape[0] // MIC
    NB = x.shape[1] // BLK
    SH = NB // Z
    groups = NB // GRP

    def rows(m):
        return pl.ds(m * MIC, MIC)

    def wait(view, sem):
        pltpu.make_async_copy(view, view, sem).wait()

    top_copy = pltpu.make_async_copy(top, ups, top_sem)

    @pl.when(is_last)
    def _():
        top_copy.start()

    barrier = pltpu.get_barrier_semaphore()
    for off in range(1, H):
        pl.semaphore_signal(barrier, 1, device_id={"hidden": lax.rem(h + off, H)}, device_id_type=MESH)
    for off in range(1, Z):
        pl.semaphore_signal(barrier, 1, device_id={"tok": lax.rem(z + off, Z)}, device_id_type=MESH)

    for peer in (below, above):
        pl.semaphore_signal(barrier, 1, device_id={"section": peer}, device_id_type=MESH)

    mine = pl.ds(z * SH, SH)
    for s in range(SH):
        weights[LS, z * SH + s] = ls[s].astype(F32).T.astype(BF)
    weights[RF, mine] = rf[...]
    weights[LF, mine] = lf[...]
    weights[RS, mine] = rs[...]

    pl.semaphore_wait(barrier, H - 1 + Z - 1 + 2)

    for f in (RF, LF, LS, RS):
        for off in range(1, Z):
            pltpu.make_async_remote_copy(
                src_ref=weights.at[f, mine],
                dst_ref=weights.at[f, mine],
                send_sem=w_send.at[f],
                recv_sem=w_recv.at[f],
                device_id={"tok": lax.rem(z + off, Z)},
                device_id_type=MESH,
            ).start()

    for f in range(4):
        sums[f] = jnp.zeros_like(sums[f])

    def wait_weights(f):
        wait(weights.at[f, pl.ds(0, (Z - 1) * SH)], w_recv.at[f])

    def over_groups(body, before=None, after=None):
        def group(g, carry):
            if before is not None:
                before(g)
            for u in range(GRP):
                body(g * GRP + u)
            if after is not None:
                after(g)
            return carry

        lax.fori_loop(0, groups, group, 0)

    def put(block, value):
        stage[pl.ds(block, BLK, stride=NB), :] = value

    def staged(d):
        part = pl.ds(pl.multiple_of(d * NB * NB, NB * NB), NB * NB)
        return stage[part, :].astype(BF).reshape(NB, NB, MIC)

    def exchange(p, m):
        slot = pl.ds(pl.multiple_of(h * NB, NB), NB)
        for off in sorted(range(1, H), key=lambda o: abs(o - H // 2)):
            peer = lax.rem(h + off, H)
            send[p, m, peer] = staged(peer)
            pltpu.make_async_remote_copy(
                src_ref=send.at[p, m, peer],
                dst_ref=recv.at[p, m, :, slot, :],
                send_sem=a_send.at[p, m],
                recv_sem=a_recv.at[p, m],
                device_id={"hidden": peer},
                device_id_type=MESH,
            ).start()
        recv[p, m, :, slot, :] = staged(h)

    def wait_exchange(p, m):
        wait(recv.at[p, m, pl.ds(0, NB - NB // H)], a_recv.at[p, m])

    def first_mid(m):
        over_groups(lambda b: put(b, nt(weights[RF, b], x[rows(m), lanes(b)])))
        exchange(FM, m)

    def activations(m):
        def body(j):
            a, d = gelu_parts(nn(weights[LF, j], recv[FM, m, j]))
            act[m, j] = a.astype(BF)
            der[m, j] = d

        wait_exchange(FM, m)
        over_groups(body)

    def second_mid(m):
        over_groups(lambda b: put(b, nn(weights[RS, b], act[m, b])))
        exchange(SM, m)

    def grad_mid_second(m, arrives):
        def before(g):
            wait(ups.at[rows(m), lanes(g * GRP, GRP)], p_recv.at[m, g])

        over_groups(
            lambda j: put(j, nt(weights[LS, j], ups[rows(m), lanes(j)])),
            before=before if arrives else None,
        )
        exchange(GM2, m)

    def grad_mid_first(m):
        def body(b):
            pre = (nn(turned[1, b], recv[GM2, m, b]) * der[m, b]).astype(BF)
            gpre[m, b] = pre
            put(b, nn(turned[0, b], pre))

        wait_exchange(GM2, m)
        over_groups(body)
        exchange(GM1, m)

    def input_adjoint(m):
        def body(b):
            at = lanes(b)
            grad = tn(recv[GM1, m, b], weights[RF, b])
            adj[rows(m), at] = (ups[rows(m), at].astype(F32) + grad).astype(BF)

        def after(g):
            @pl.when(jnp.logical_not(is_first))
            def _():
                part = lanes(g * GRP, GRP)
                pltpu.make_async_remote_copy(
                    src_ref=adj.at[rows(m), part],
                    dst_ref=ups.at[rows(m), part],
                    send_sem=p_send.at[m, g],
                    recv_sem=p_recv.at[m, g],
                    device_id={"section": below},
                    device_id_type=MESH,
                ).start()

        wait_exchange(GM1, m)
        over_groups(body, after=after)

    def wide_gradients(m):
        def body(b):
            sums[RS, b] += nt(recv[GM2, m, b], act[m, b])
            sums[LF, b] += nt(gpre[m, b], recv[FM, m, b])

        over_groups(body)

    def gradient_rf(m):
        def body(b):
            sums[RF, b] += nn(recv[GM1, m, b], x[rows(m), lanes(b)])

        over_groups(body)

    def gradient_ls(m):
        def body(j):
            sums[LS, j] += nn(recv[SM, m, j], ups[rows(m), lanes(j)])

        wait_exchange(SM, m)
        over_groups(body)

    def scatter(f):
        for off in range(1, Z):
            peer = lax.rem(z + off, Z)
            theirs = pl.ds(peer * SH, SH)
            part_send[f, theirs] = sums[f, theirs].astype(BF)
            pltpu.make_async_remote_copy(
                src_ref=part_send.at[f, theirs],
                dst_ref=part_recv.at[f, z],
                send_sem=r_send.at[f],
                recv_sem=r_recv.at[f],
                device_id={"tok": peer},
                device_id_type=MESH,
            ).start()

    def collect(f, out, turn=False):
        wait(part_recv.at[f, pl.ds(0, Z - 1)], r_recv.at[f])
        for s in range(SH):
            total = sums[f, z * SH + s]
            for off in range(1, Z):
                total = total + part_recv[f, lax.rem(z + off, Z), s].astype(F32)
            total = scale * total
            out[s] = total.T if turn else total

    wait_weights(RF)
    for m in range(M):
        first_mid(m)
    wait_weights(LF)
    wait_weights(LS)

    @pl.when(is_last)
    def _():
        top_copy.wait()
        for m in range(M):
            grad_mid_second(m, False)

    wait_weights(RS)

    def turn(b):
        turned[0, b] = weights[LF, b].astype(F32).T.astype(BF)
        turned[1, b] = weights[RS, b].astype(F32).T.astype(BF)

    over_groups(turn)
    for m in range(M):
        activations(m)

        @pl.when(jnp.logical_not(is_last))
        def _():
            second_mid(m)

    def begin(m):
        @pl.when(jnp.logical_not(is_last))
        def _():
            grad_mid_second(m, True)
            gradient_ls(m)

    begin(0)
    for m in range(M):
        grad_mid_first(m)
        wide_gradients(m)
        if m + 1 < M:
            begin(m + 1)
        else:
            scatter(RS)
            scatter(LF)
        input_adjoint(m)
        gradient_rf(m)
    scatter(RF)

    @pl.when(is_last)
    def _():
        for m in range(M):
            second_mid(m)
        for m in range(M):
            gradient_ls(m)

    scatter(LS)
    collect(RS, o_rs)
    collect(LF, o_lf)
    collect(RF, o_rf)
    collect(LS, o_ls, True)

    for f in range(4):
        wait(weights.at[f, pl.ds(0, (Z - 1) * SH)], w_send.at[f])
        wait(part_send.at[f, pl.ds(0, (Z - 1) * SH)], r_send.at[f])
    for p in range(4):
        for m in range(M):
            wait(send.at[p, m, pl.ds(0, H - 1)], a_send.at[p, m])

    @pl.when(jnp.logical_not(is_first))
    def _():
        for m in range(M):
            for g in range(groups):
                wait(adj.at[rows(m), lanes(g * GRP, GRP)], p_send.at[m, g])


def solution(mesh):
    S, H, Z = (mesh.shape[name] for name in ("section", "hidden", "tok"))

    def on_device(section_inputs, top_adjoint, right_first, left_first, right_second, left_second):
        tokens, width = top_adjoint.shape
        M, NB, SH = tokens // MIC, width // BLK, right_first.shape[1]
        groups = NB // GRP
        scale = 1.0 / math.sqrt(tokens * Z)
        vmem = pl.BlockSpec(memory_space=pltpu.VMEM)
        dma = pltpu.SemaphoreType.DMA
        shard = jax.ShapeDtypeStruct((SH, BLK, BLK), F32)
        outs = pl.pallas_call(
            functools.partial(kernel, S, H, Z, scale),
            out_shape=[jax.ShapeDtypeStruct((tokens, width), BF)] + [shard] * 4,
            in_specs=[vmem, pl.BlockSpec(memory_space=pl.ANY)] + [vmem] * 4,
            out_specs=[vmem] * 5,
            scratch_shapes=[
                pltpu.VMEM((tokens, width), BF),
                pltpu.VMEM((4, M, H, NB, NB, MIC), BF),
                pltpu.VMEM((4, M, NB, BLK, MIC), BF),
                pltpu.VMEM((M, NB, BLK, MIC), BF),
                pltpu.VMEM((M, NB, BLK, MIC), F32),
                pltpu.VMEM((M, NB, BLK, MIC), BF),
                pltpu.VMEM((NB * BLK, MIC), F32),
                pltpu.VMEM((4, NB, BLK, BLK), BF),
                pltpu.VMEM((2, NB, BLK, BLK), BF),
                pltpu.VMEM((4, NB, BLK, BLK), F32),
                pltpu.VMEM((4, NB, BLK, BLK), BF),
                pltpu.VMEM((4, Z, SH, BLK, BLK), BF),
                dma,
                dma((4,)),
                dma((4,)),
                dma((4, M)),
                dma((4, M)),
                dma((M, groups)),
                dma((M, groups)),
                dma((4,)),
                dma((4,)),
            ],
            compiler_params=pltpu.CompilerParams(
                collective_id=0, has_side_effects=True, vmem_limit_bytes=56 * 1024 * 1024
            ),
        )(section_inputs[0], top_adjoint, right_first[0], left_first[0], right_second[0], left_second[0])
        return tuple(o[None] for o in outs)

    act = P("section", "tok", "hidden")
    weight = P("section", ("hidden", "tok"), None, None)
    return jax.shard_map(
        on_device,
        mesh=mesh,
        in_specs=(act, P("tok", "hidden"), weight, weight, weight, weight),
        out_specs=(act, weight, weight, weight, weight),
        check_vma=False,
    )
```

time: 620 us -> 241 us (0.39); the launches traced: 613 us -> 241 us
  waiting for transfers between devices: 271 us -> 0 us
  Pallas kernels: 0 us -> 235 us
  starting transfers between devices: 96.9 us -> 0 us
  blocking collectives: 86.6 us -> 0 us
  local copies, waits for them, and re-layouts: 60.4 us -> 5.42 us
  other arithmetic: 45.2 us -> 0 us
  matrix products: 38.4 us -> 0 us
  between operations: 13.9 us -> 0.68 us
    pallas_call x0 -> x1, Pallas kernels: none -> 235 us  [on_device(): pl.pallas_call(functools.partial(kernel, S, H, Z, scale), out_shape=[jax....]
    all_to_all x14 -> x0, waiting for transfers between devices: 108 us -> none  [swap_blocks(): lax.all_to_all(values, 'hidden', split_axis=0, concat_axis=1, tiled=True)]
    reduce_scatter x4 -> x0, waiting for transfers between devices: 104 us -> none  [on_device(): lax.psum_scatter(g.astype(bf), 'tok', scatter_dimension=0, tiled=True)]
    all_to_all x14 -> x0, starting transfers between devices: 89 us -> none  [swap_blocks(): lax.all_to_all(values, 'hidden', split_axis=0, concat_axis=1, tiled=True)]
    all_gather x4 -> x0, blocking collectives: 86.6 us -> none  [on_device(): lax.all_gather(w[0], 'tok', axis=0, tiled=True)]
    ppermute x6 -> x0, waiting for transfers between devices: 58.5 us -> none  [passed_along(): return lax.ppermute(block, axis, route)]
    dynamic_update_slice x18 -> x0, other arithmetic: 38.6 us -> none  [keep(): lax.dynamic_update_slice_in_dim(whole, jnp.where(active, part, old), star...]
    dot_general x31 -> x0, matrix products: 38.4 us -> none  [dot(): return jnp.einsum(spec, a, b, preferred_element_type=jnp.float32)]
  transfers between devices with their start and end apart: 24 -> 0, of which waited for: 22 -> 0; matrix products, arithmetic and copies ran while one was open for 10% -> 0% of each run, Pallas kernels for 0% -> 0%
where the time goes in v2:
time: 241 us
  Pallas kernels  235 us (98%)
  local copies, waits for them, and re-layouts  5.42 us (2%)
    pallas_call x1, Pallas kernels, on_device(): pl.pallas_call(functools.partial(kernel, S, H, Z, scale), out_shape=[jax....  235 us
    unnamed x13, local copies, waits for them, and re-layouts  5.42 us

profile of v2, /device:TPU:1, one launch (start us, length us, event | category | flops | bytes accessed | tf_op | source)
XLA Modules:
  0.0 241.2 jit_solution(10336806025088898643)
XLA Ops:
  0.6 235.1 %shard_map.101 = (bf16[384,2048]{1,0:T(8,128)(2,1)}, f32[2,128,128]{2,1,0:T(8,128)}, f32[2,128,128]{2,1,0:T(8,128)}, f32[2,128,128]{2,1,0:T(8,128)}, f32[2,128,128]{2,1,0:T(8,128)}) custom-call(bf16[384,2048]{1,0:T(8,128)(2,1)} %bitcast.11, bf16[384,2048]{1,0:T(8,128)(2,1)} %top.1, bf16[2,128,128]{2,1,0:T(8,128)(2,1)} %bitcast.16, ...), custom_call_target="tpu_custom_call" | custom-call | tf_op jit(solution)/shard_map/pallas_call | solution.py:330
  235.7 0.0 copy-start.3
  235.8 0.0 copy-start.2
  235.8 0.0 copy-start.1
  235.8 0.0 copy-start
  235.8 2.8 %copy.16 = bf16[1,384,2048]{2,1,0:T(8,128)(2,1)} copy(bf16[1,384,2048]{2,1,0:T(8,128)(2,1)} %bitcast.10) | data formatting | bytes 3145728
  238.6 0.0 copy-done.3
  238.6 0.7 copy.17
  239.2 0.0 copy-done.2
  239.2 0.7 copy.18
  239.9 0.0 copy-done.1
  239.9 0.7 copy.19
  240.5 0.0 copy-done
  240.5 0.7 copy.20
Async XLA Ops:
  235.7 2.8 %copy-start.3 = (f32[2,128,128]{2,1,0:T(8,128)S(1)}, f32[2,128,128]{2,1,0:T(8,128)}, u32[]{:S(2)}) copy-start(f32[2,128,128]{2,1,0:T(8,128)} %get-tuple-element.11) | copy-start | bytes 393220
  235.8 3.5 %copy-start.2 = (f32[2,128,128]{2,1,0:T(8,128)S(1)}, f32[2,128,128]{2,1,0:T(8,128)}, u32[]{:S(2)}) copy-start(f32[2,128,128]{2,1,0:T(8,128)} %get-tuple-element.12) | copy-start | bytes 393220
  235.8 4.1 %copy-start.1 = (f32[2,128,128]{2,1,0:T(8,128)S(1)}, f32[2,128,128]{2,1,0:T(8,128)}, u32[]{:S(2)}) copy-start(f32[2,128,128]{2,1,0:T(8,128)} %get-tuple-element.13) | copy-start | bytes 393220
  235.8 4.8 %copy-start = (f32[2,128,128]{2,1,0:T(8,128)S(1)}, f32[2,128,128]{2,1,0:T(8,128)}, u32[]{:S(2)}) copy-start(f32[2,128,128]{2,1,0:T(8,128)} %get-tuple-element.14) | copy-start | bytes 393220

commit v3 on v2

--- a/solution.py
+++ b/solution.py
@@ -86,24 +86,73 @@
     weights[LF, mine] = lf[...]
     weights[RS, mine] = rs[...]
 
-    pl.semaphore_wait(barrier, H - 1 + Z - 1 + 2)
-
-    for f in (RF, LF, LS, RS):
-        for off in range(1, Z):
-            pltpu.make_async_remote_copy(
-                src_ref=weights.at[f, mine],
-                dst_ref=weights.at[f, mine],
-                send_sem=w_send.at[f],
-                recv_sem=w_recv.at[f],
-                device_id={"tok": lax.rem(z + off, Z)},
-                device_id_type=MESH,
-            ).start()
-
     for f in range(4):
         sums[f] = jnp.zeros_like(sums[f])
 
-    def wait_weights(f):
-        wait(weights.at[f, pl.ds(0, (Z - 1) * SH)], w_recv.at[f])
+    pl.semaphore_wait(barrier, H - 1 + Z - 1 + 2)
+
+    def hops(f, way):
+        return Z // 2 if way == f % 2 else Z - 1 - Z // 2
+
+    def next_on(way):
+        return {"tok": lax.rem(z + (1 if way == 0 else Z - 1), Z)}
+
+    def ahead(way, distance):
+        return lax.rem(z + (distance if way == 0 else Z - distance), Z)
+
+    def share(index):
+        return pl.ds(index * SH, SH)
+
+    def gather_step(f, k):
+        for way in (0, 1):
+            if k < hops(f, way):
+                part = weights.at[f, share(ahead(1 - way, k) if k else z)]
+                if k:
+                    wait(part, w_recv.at[f, way, k - 1])
+                pltpu.make_async_remote_copy(
+                    src_ref=part,
+                    dst_ref=part,
+                    send_sem=w_send.at[f],
+                    recv_sem=w_recv.at[f, way, k],
+                    device_id=next_on(way),
+                    device_id_type=MESH,
+                ).start()
+
+    def gather_end(f):
+        for way in (0, 1):
+            wait(weights.at[f, share(0)], w_recv.at[f, way, hops(f, way) - 1])
+
+    def scatter_step(f, k):
+        for way in (0, 1):
+            n = hops(f, way)
+            if k < n:
+                target = ahead(way, n - k)
+                if k:
+                    wait(part_recv.at[f, way, k - 1], r_recv.at[f, way, k - 1])
+                for s in range(SH):
+                    total = sums[f, target * SH + s]
+                    if k:
+                        total = total + part_recv[f, way, k - 1, s].astype(F32)
+                    part_send[f, way, k, s] = total.astype(BF)
+                pltpu.make_async_remote_copy(
+                    src_ref=part_send.at[f, way, k],
+                    dst_ref=part_recv.at[f, way, k],
+                    send_sem=r_send.at[f],
+                    recv_sem=r_recv.at[f, way, k],
+                    device_id=next_on(way),
+                    device_id_type=MESH,
+                ).start()
+
+    def collect(f, out, turn=False):
+        for way in (0, 1):
+            last = hops(f, way) - 1
+            wait(part_recv.at[f, way, last], r_recv.at[f, way, last])
+        for s in range(SH):
+            total = sums[f, z * SH + s]
+            for way in (0, 1):
+                total = total + part_recv[f, way, hops(f, way) - 1, s].astype(F32)
+            total = scale * total
+            out[s] = total.T if turn else total
 
     def over_groups(body, before=None, after=None):
         def group(g, carry):
@@ -120,27 +169,36 @@
     def put(block, value):
         stage[pl.ds(block, BLK, stride=NB), :] = value
 
-    def staged(d):
-        part = pl.ds(pl.multiple_of(d * NB * NB, NB * NB), NB * NB)
-        return stage[part, :].astype(BF).reshape(NB, NB, MIC)
+    slot = pl.ds(pl.multiple_of(h * NB, NB), NB)
+
+    def staged(d, g):
+        at = pl.multiple_of((d * NB + g * GRP) * NB, NB)
+        return stage[pl.ds(at, GRP * NB), :].astype(BF).reshape(GRP, NB, MIC)
 
     def exchange(p, m):
-        slot = pl.ds(pl.multiple_of(h * NB, NB), NB)
-        for off in sorted(range(1, H), key=lambda o: abs(o - H // 2)):
-            peer = lax.rem(h + off, H)
-            send[p, m, peer] = staged(peer)
-            pltpu.make_async_remote_copy(
-                src_ref=send.at[p, m, peer],
-                dst_ref=recv.at[p, m, :, slot, :],
-                send_sem=a_send.at[p, m],
-                recv_sem=a_recv.at[p, m],
-                device_id={"hidden": peer},
-                device_id_type=MESH,
-            ).start()
-        recv[p, m, :, slot, :] = staged(h)
-
-    def wait_exchange(p, m):
-        wait(recv.at[p, m, pl.ds(0, NB - NB // H)], a_recv.at[p, m])
+        def quarter(g, carry):
+            part = pl.ds(g * GRP, GRP)
+            for off in sorted(range(1, H), key=lambda o: abs(o - H // 2)):
+                peer = lax.rem(h + off, H)
+                send[p, m, peer, part] = staged(peer, g)
+                pltpu.make_async_remote_copy(
+                    src_ref=send.at[p, m, peer, part],
+                    dst_ref=recv.at[p, m, part, slot, :],
+                    send_sem=a_send.at[p, m],
+                    recv_sem=a_recv.at[p, m, g],
+                    device_id={"hidden": peer},
+                    device_id_type=MESH,
+                ).start()
+            recv[p, m, part, slot, :] = staged(h, g)
+            return carry
+
+        lax.fori_loop(0, groups, quarter, 0)
+
+    def arrival(p, m):
+        def before(g):
+            wait(recv.at[p, m, pl.ds(g * GRP, GRP), pl.ds(0, BLK - NB)], a_recv.at[p, m, g])
+
+        return before
 
     def first_mid(m):
         over_groups(lambda b: put(b, nt(weights[RF, b], x[rows(m), lanes(b)])))
@@ -152,8 +210,7 @@
             act[m, j] = a.astype(BF)
             der[m, j] = d
 
-        wait_exchange(FM, m)
-        over_groups(body)
+        over_groups(body, before=arrival(FM, m))
 
     def second_mid(m):
         over_groups(lambda b: put(b, nn(weights[RS, b], act[m, b])))
@@ -175,8 +232,7 @@
             gpre[m, b] = pre
             put(b, nn(turned[0, b], pre))
 
-        wait_exchange(GM2, m)
-        over_groups(body)
+        over_groups(body, before=arrival(GM2, m))
         exchange(GM1, m)
 
     def input_adjoint(m):
@@ -198,8 +254,7 @@
                     device_id_type=MESH,
                 ).start()
 
-        wait_exchange(GM1, m)
-        over_groups(body, after=after)
+        over_groups(body, before=arrival(GM1, m), after=after)
 
     def wide_gradients(m):
         def body(b):
@@ -218,93 +273,120 @@
         def body(j):
             sums[LS, j] += nn(recv[SM, m, j], ups[rows(m), lanes(j)])
 
-        wait_exchange(SM, m)
-        over_groups(body)
-
-    def scatter(f):
-        for off in range(1, Z):
-            peer = lax.rem(z + off, Z)
-            theirs = pl.ds(peer * SH, SH)
-            part_send[f, theirs] = sums[f, theirs].astype(BF)
-            pltpu.make_async_remote_copy(
-                src_ref=part_send.at[f, theirs],
-                dst_ref=part_recv.at[f, z],
-                send_sem=r_send.at[f],
-                recv_sem=r_recv.at[f],
-                device_id={"tok": peer},
-                device_id_type=MESH,
-            ).start()
-
-    def collect(f, out, turn=False):
-        wait(part_recv.at[f, pl.ds(0, Z - 1)], r_recv.at[f])
-        for s in range(SH):
-            total = sums[f, z * SH + s]
-            for off in range(1, Z):
-                total = total + part_recv[f, lax.rem(z + off, Z), s].astype(F32)
-            total = scale * total
-            out[s] = total.T if turn else total
-
-    wait_weights(RF)
-    for m in range(M):
-        first_mid(m)
-    wait_weights(LF)
-    wait_weights(LS)
-
-    @pl.when(is_last)
-    def _():
-        top_copy.wait()
-        for m in range(M):
-            grad_mid_second(m, False)
-
-    wait_weights(RS)
+        over_groups(body, before=arrival(SM, m))
 
     def turn(b):
         turned[0, b] = weights[LF, b].astype(F32).T.astype(BF)
         turned[1, b] = weights[RS, b].astype(F32).T.astype(BF)
 
-    over_groups(turn)
-    for m in range(M):
-        activations(m)
-
-        @pl.when(jnp.logical_not(is_last))
-        def _():
+    steps = Z // 2
+    for k in range(steps):
+        gather_step(RF, k)
+        gather_step(LS, k)
+    gather_step(LF, 0)
+    gather_step(RS, 0)
+    gather_end(RF)
+    gather_end(LS)
+
+    def more(k):
+        for f in (LF, RS):
+            if k < steps:
+                gather_step(f, k)
+            else:
+                gather_end(f)
+
+    def chain_of_last():
+        top_copy.wait()
+        first_mid(0)
+        grad_mid_second(0, False)
+        more(1)
+        first_mid(1)
+        grad_mid_second(1, False)
+        more(2)
+        more(3)
+        more(4)
+        over_groups(turn)
+        activations(0)
+        grad_mid_first(0)
+        first_mid(2)
+        grad_mid_second(2, False)
+        activations(1)
+        grad_mid_first(1)
+        input_adjoint(0)
+        activations(2)
+        grad_mid_first(2)
+        input_adjoint(1)
+        wide_gradients(0)
+        input_adjoint(2)
+        for m in range(M):
             second_mid(m)
-
-    def begin(m):
-        @pl.when(jnp.logical_not(is_last))
-        def _():
+        gradient_rf(0)
+        for m in range(1, M):
+            wide_gradients(m)
+            gradient_rf(m)
+        for m in range(M):
+            gradient_ls(m)
+        for f in (RS, LF, LS):
+            scatter_step(f, 0)
+        for f in (RS, LF, LS):
+            scatter_step(f, 1)
+
+    def chain_of_others():
+        for m in range(M):
+            first_mid(m)
+            more(m + 1)
+        gather_end(LF)
+        activations(0)
+        gather_end(RS)
+        second_mid(0)
+        for m in range(1, M):
+            activations(m)
+            second_mid(m)
+        over_groups(turn)
+
+        def begin(m):
             grad_mid_second(m, True)
             gradient_ls(m)
 
-    begin(0)
-    for m in range(M):
-        grad_mid_first(m)
-        wide_gradients(m)
-        if m + 1 < M:
-            begin(m + 1)
-        else:
-            scatter(RS)
-            scatter(LF)
-        input_adjoint(m)
-        gradient_rf(m)
-    scatter(RF)
-
-    @pl.when(is_last)
-    def _():
-        for m in range(M):
-            second_mid(m)
-        for m in range(M):
-            gradient_ls(m)
-
-    scatter(LS)
+        begin(0)
+        for m in range(M):
+            grad_mid_first(m)
+            if m + 1 == M:
+                scatter_step(LS, 0)
+            wide_gradients(m)
+            if m + 1 < M:
+                begin(m + 1)
+            else:
+                scatter_step(RS, 0)
+                scatter_step(LF, 0)
+                scatter_step(LS, 1)
+            input_adjoint(m)
+            if m + 1 == M:
+                scatter_step(RS, 1)
+                scatter_step(LF, 1)
+            gradient_rf(m)
+
+    pl.when(is_last)(chain_of_last)
+    pl.when(jnp.logical_not(is_last))(chain_of_others)
+
+    scatter_step(RF, 0)
+    scatter_step(LS, 2)
+    scatter_step(RS, 2)
+    scatter_step(LF, 2)
+    scatter_step(RF, 1)
+    scatter_step(LS, 3)
+    scatter_step(RS, 3)
+    scatter_step(LF, 3)
+    scatter_step(RF, 2)
+    collect(LS, o_ls, True)
+    scatter_step(RF, 3)
     collect(RS, o_rs)
     collect(LF, o_lf)
     collect(RF, o_rf)
-    collect(LS, o_ls, True)
 
     for f in range(4):
         wait(weights.at[f, pl.ds(0, (Z - 1) * SH)], w_send.at[f])
-        wait(part_send.at[f, pl.ds(0, (Z - 1) * SH)], r_send.at[f])
+        wait(weights.at[f, pl.ds(0, (Z - 1) * SH)], r_send.at[f])
     for p in range(4):
         for m in range(M):
             wait(send.at[p, m, pl.ds(0, H - 1)], a_send.at[p, m])
@@ -343,17 +425,17 @@
                 pltpu.VMEM((4, NB, BLK, BLK), BF),
                 pltpu.VMEM((2, NB, BLK, BLK), BF),
                 pltpu.VMEM((4, NB, BLK, BLK), F32),
-                pltpu.VMEM((4, NB, BLK, BLK), BF),
-                pltpu.VMEM((4, Z, SH, BLK, BLK), BF),
+                pltpu.VMEM((4, 2, Z // 2, SH, BLK, BLK), BF),
+                pltpu.VMEM((4, 2, Z // 2, SH, BLK, BLK), BF),
                 dma,
                 dma((4,)),
-                dma((4,)),
+                dma((4, 2, Z // 2)),
                 dma((4, M)),
-                dma((4, M)),
+                dma((4, M, groups)),
                 dma((M, groups)),
                 dma((M, groups)),
                 dma((4,)),
-                dma((4,)),
+                dma((4, 2, Z // 2)),
             ],
             compiler_params=pltpu.CompilerParams(
                 collective_id=0, has_side_effects=True, vmem_limit_bytes=56 * 1024 * 1024

time: 241 us -> 197 us (0.82)
  Pallas kernels: 235 us -> 190 us
    pallas_call x1, Pallas kernels: 235 us -> 190 us  [on_device(): pl.pallas_call(functools.partial(kernel, S, H, Z, scale), out_shape=[jax....]
where the time goes in v3:
time: 197 us; the launch traced here: 196 us
  Pallas kernels  190 us (96%)
  local copies, waits for them, and re-layouts  5.42 us (3%)
    pallas_call x1, Pallas kernels, on_device(): pl.pallas_call(functools.partial(kernel, S, H, Z, scale), out_shape=[jax....  190 us
    unnamed x13, local copies, waits for them, and re-layouts  5.42 us

profile of v3, /device:TPU:1, one launch (start us, length us, event | category | flops | bytes accessed | tf_op | source)
XLA Modules:
  0.0 196.0 jit_solution(6558903735638771382)
XLA Ops:
  0.6 189.9 %shard_map.101 = (bf16[384,2048]{1,0:T(8,128)(2,1)}, f32[2,128,128]{2,1,0:T(8,128)}, f32[2,128,128]{2,1,0:T(8,128)}, f32[2,128,128]{2,1,0:T(8,128)}, f32[2,128,128]{2,1,0:T(8,128)}) custom-call(bf16[384,2048]{1,0:T(8,128)(2,1)} %bitcast.11, bf16[384,2048]{1,0:T(8,128)(2,1)} %top.1, bf16[2,128,128]{2,1,0:T(8,128)(2,1)} %bitcast.16, ...), custom_call_target="tpu_custom_call" | custom-call | tf_op jit(solution)/shard_map/pallas_call | solution.py:412
  190.5 0.0 copy-start.3
  190.5 0.0 copy-start.2
  190.5 0.0 copy-start.1
  190.6 0.0 copy-start
  190.6 2.8 %copy.16 = bf16[1,384,2048]{2,1,0:T(8,128)(2,1)} copy(bf16[1,384,2048]{2,1,0:T(8,128)(2,1)} %bitcast.10) | data formatting | bytes 3145728
  193.3 0.0 copy-done.3
  193.4 0.7 copy.17
  194.0 0.0 copy-done.2
  194.0 0.7 copy.18
  194.7 0.0 copy-done.1
  194.7 0.7 copy.19
  195.3 0.0 copy-done
  195.3 0.7 copy.20
Async XLA Ops:
  190.5 2.8 %copy-start.3 = (f32[2,128,128]{2,1,0:T(8,128)S(1)}, f32[2,128,128]{2,1,0:T(8,128)}, u32[]{:S(2)}) copy-start(f32[2,128,128]{2,1,0:T(8,128)} %get-tuple-element.11) | copy-start | bytes 393220
  190.5 3.5 %copy-start.2 = (f32[2,128,128]{2,1,0:T(8,128)S(1)}, f32[2,128,128]{2,1,0:T(8,128)}, u32[]{:S(2)}) copy-start(f32[2,128,128]{2,1,0:T(8,128)} %get-tuple-element.12) | copy-start | bytes 393220
  190.5 4.1 %copy-start.1 = (f32[2,128,128]{2,1,0:T(8,128)S(1)}, f32[2,128,128]{2,1,0:T(8,128)}, u32[]{:S(2)}) copy-start(f32[2,128,128]{2,1,0:T(8,128)} %get-tuple-element.13) | copy-start | bytes 393220
  190.6 4.8 %copy-start = (f32[2,128,128]{2,1,0:T(8,128)S(1)}, f32[2,128,128]{2,1,0:T(8,128)}, u32[]{:S(2)}) copy-start(f32[2,128,128]{2,1,0:T(8,128)} %get-tuple-element.14) | copy-start | bytes 393220

commit v4 on v3

v4 whole, which is shorter than its diff:
```python
import functools
import math

import jax
import jax.numpy as jnp
from jax import lax
from jax.experimental import pallas as pl
from jax.experimental.pallas import tpu as pltpu
from jax.sharding import PartitionSpec as P

MESH = pl.DeviceIdType.MESH
BF, F32 = jnp.bfloat16, jnp.float32
BLK = 128
MIC = 64
LANES = 2 * MIC
GRP = 4
COEF = 0.7978845608028654
FM, SM, GM2, GM1 = range(4)
RF, LF, RS, LS = range(4)


def gelu_parts(v):
    squashed = jnp.tanh(COEF * (v + 0.044715 * v * v * v))
    activation = 0.5 * v * (1.0 + squashed)
    derivative = 0.5 * (1.0 + squashed) + 0.5 * v * (1.0 - squashed * squashed) * COEF * (
        1.0 + 3.0 * 0.044715 * v * v
    )
    return activation, derivative


def nn(a, b):
    return lax.dot_general(a, b, (((1,), (0,)), ((), ())), preferred_element_type=F32)


def nt(a, b):
    return lax.dot_general(a, b, (((1,), (1,)), ((), ())), preferred_element_type=F32)


def tn(a, b):
    return lax.dot_general(a, b, (((0,), (0,)), ((), ())), preferred_element_type=F32)


def lanes(b, count=1):
    return pl.ds(pl.multiple_of(b * BLK, BLK), count * BLK)


def kernel(
    S, H, Z, scale,
    x, top, rf, lf, rs, ls,
    adj, grads,
    ups, send, recv, act, der, gpre, stage, weights, turned, sums, part_send, part_recv,
    top_sem, w_send, w_recv, a_send, a_recv, p_send, p_recv, r_send, r_recv,
):
    sec, h, z = (lax.axis_index(name) for name in ("section", "hidden", "tok"))
    is_last, is_first = sec == S - 1, sec == 0
    early = sec < S - 2
    below, above = lax.rem(sec + S - 1, S), lax.rem(sec + 1, S)
    M = x.shape[0] // MIC
    NB = x.shape[1] // BLK
    SH = NB // Z
    half = NB // 2
    groups = half // GRP

    def rows(m):
        return pl.ds(pl.multiple_of(m * MIC, MIC), MIC)

    def wait(view, sem):
        pltpu.make_async_copy(view, view, sem).wait()

    top_copy = pltpu.make_async_copy(top, ups, top_sem)

    @pl.when(is_last)
    def _():
        top_copy.start()

    barrier = pltpu.get_barrier_semaphore()
    for off in range(1, H):
        pl.semaphore_signal(barrier, 1, device_id={"hidden": lax.rem(h + off, H)}, device_id_type=MESH)
    for off in range(1, Z):
        pl.semaphore_signal(barrier, 1, device_id={"tok": lax.rem(z + off, Z)}, device_id_type=MESH)

    for peer in (below, above):
        pl.semaphore_signal(barrier, 1, device_id={"section": peer}, device_id_type=MESH)

    mine = pl.ds(z * SH, SH)
    for s in range(SH):
        weights[LS, z * SH + s] = ls[s].astype(F32).T.astype(BF)
    weights[RF, mine] = rf[...]
    weights[LF, mine] = lf[...]
    weights[RS, mine] = rs[...]

    for f in range(4):
        sums[f] = jnp.zeros_like(sums[f])

    pl.semaphore_wait(barrier, H - 1 + Z - 1 + 2)

    def hops(f, way):
        return Z // 2 if way == f % 2 else Z - 1 - Z // 2

    def next_on(way):
        return {"tok": lax.rem(z + (1 if way == 0 else Z - 1), Z)}

    def ahead(way, distance):
        return lax.rem(z + (distance if way == 0 else Z - distance), Z)

    def share(index):
        return pl.ds(index * SH, SH)

    def gather_step(f, k):
        for way in (0, 1):
            if k < hops(f, way):
                part = weights.at[f, share(ahead(1 - way, k) if k else z)]
                if k:
                    wait(part, w_recv.at[f, way, k - 1])
                pltpu.make_async_remote_copy(
                    src_ref=part,
                    dst_ref=part,
                    send_sem=w_send.at[f],
                    recv_sem=w_recv.at[f, way, k],
                    device_id=next_on(way),
                    device_id_type=MESH,
                ).start()

    def gather_end(f):
        for way in (0, 1):
            wait(weights.at[f, share(0)], w_recv.at[f, way, hops(f, way) - 1])

    def scatter_step(f, k):
        for way in (0, 1):
            n = hops(f, way)
            if k < n:
                target = ahead(way, n - k)
                if k:
                    wait(part_recv.at[f, way, k - 1], r_recv.at[f, way, k - 1])
                for s in range(SH):
                    total = sums[f, target * SH + s]
                    if k:
                        total = total + part_recv[f, way, k - 1, s].astype(F32)
                    part_send[f, way, k, s] = total.astype(BF)
                pltpu.make_async_remote_copy(
                    src_ref=part_send.at[f, way, k],
                    dst_ref=part_recv.at[f, way, k],
                    send_sem=r_send.at[f],
                    recv_sem=r_recv.at[f, way, k],
                    device_id=next_on(way),
                    device_id_type=MESH,
                ).start()

    def collect(f, turn=False):
        for way in (0, 1):
            last = hops(f, way) - 1
            wait(part_recv.at[f, way, last], r_recv.at[f, way, last])
        for s in range(SH):
            total = sums[f, z * SH + s]
            for way in (0, 1):
                total = total + part_recv[f, way, hops(f, way) - 1, s].astype(F32)
            total = scale * total
            grads[f, s] = total.T if turn else total

    def over_groups(body, before=None, after=None):
        def group(g, carry):
            if before is not None:
                before(g)
            for u in range(GRP):
                body(g * GRP + u)
            if after is not None:
                after(g)
            return carry

        lax.fori_loop(0, groups, group, 0)

    def low(*lead):
        shape = lead + (LANES,)
        return lax.broadcasted_iota(jnp.int32, shape, len(lead)) < MIC

    def put(block, value):
        stage[pl.ds(block, H * half, stride=NB), :] = value.reshape(H * half, LANES)

    def split(value):
        return value.reshape(H, 2, half, LANES)

    def twice(ref, m, b):
        value = ref[rows(m), lanes(b)]
        return jnp.concatenate([value, value], 0)

    def both(f, p):
        return jnp.concatenate([f[p], f[p + half]], 0)

    def diagonal(ref, m, p):
        zero = jnp.zeros((MIC, BLK), BF)
        upper = jnp.concatenate([ref[rows(m), lanes(p)], zero], 1)
        lower = jnp.concatenate([zero, ref[rows(m), lanes(p + half)]], 1)
        return jnp.concatenate([upper, lower], 0)

    def masked(value):
        zero = jnp.zeros_like(value)
        first = low(BLK)
        return jnp.concatenate([jnp.where(first, value, zero), jnp.where(first, zero, value)], 0)

    def put_narrow(weight, ref, m, p):
        for b in (p, p + half):
            out = split(nt(weight[b], twice(ref, m, b)))
            put(b, jnp.where(low(H, half), out[:, 0], out[:, 1]))

    def mine_of(value):
        return jnp.where(low(BLK), value[:BLK], value[BLK:])

    def put_wide(value, p):
        first, second, mask = split(value[:BLK]), split(value[BLK:]), low(H, half)
        other = jnp.where(mask, first[:, 1], second[:, 0]).reshape(H * half, LANES)
        other = pltpu.roll(other, MIC, 1).reshape(H, half, LANES)
        put(p, jnp.where(mask, first[:, 0], other))
        put(p + half, jnp.where(mask, other, second[:, 1]))

    slot = pl.ds(pl.multiple_of(h * NB, NB), NB)

    def staged(d, g):
        at = pl.multiple_of((d * half + g * GRP) * NB, NB)
        return stage[pl.ds(at, GRP * NB), :].astype(BF).reshape(GRP, NB, LANES)

    def exchange(p, m):
        def quarter(g, carry):
            part = pl.ds(g * GRP, GRP)
            for off in sorted(range(1, H), key=lambda o: abs(o - H // 2)):
                peer = lax.rem(h + off, H)
                send[p, m, peer, part] = staged(peer, g)
                pltpu.make_async_remote_copy(
                    src_ref=send.at[p, m, peer, part],
                    dst_ref=recv.at[p, m, part, slot, :],
                    send_sem=a_send.at[p, m],
                    recv_sem=a_recv.at[p, m, g],
                    device_id={"hidden": peer},
                    device_id_type=MESH,
                ).start()
            recv[p, m, part, slot, :] = staged(h, g)
            return carry

        lax.fori_loop(0, groups, quarter, 0)

    def arrival(p, m):
        def before(g):
            wait(recv.at[p, m, pl.ds(g * GRP, GRP), pl.ds(0, BLK - NB)], a_recv.at[p, m, g])

        return before

    def first_mid(m):
        over_groups(lambda p: put_narrow(weights.at[RF], x, m, p))
        exchange(FM, m)

    def activations(m):
        def body(p):
            a, d = gelu_parts(mine_of(nn(both(weights.at[LF], p), recv[FM, m, p])))
            act[m, p] = a.astype(BF)
            der[m, p] = d

        over_groups(body, before=arrival(FM, m))

    def second_mid(m):
        over_groups(lambda p: put_wide(nn(both(weights.at[RS], p), act[m, p]), p))
        exchange(SM, m)

    def passed(m, g, q):
        return rows(m), lanes(q * half + g * GRP, GRP)

    def grad_mid_second(m, arrives):
        def before(g):
            for q in (0, 1):
                wait(ups.at[passed(m, g, q)], p_recv.at[m, g, q])

        over_groups(
            lambda p: put_narrow(weights.at[LS], ups, m, p),
            before=before if arrives else None,
        )
        exchange(GM2, m)

    def grad_mid_first(m):
        def body(p):
            grad = mine_of(nn(both(turned.at[1], p), recv[GM2, m, p]))
            pre = (grad * der[m, p]).astype(BF)
            gpre[m, p] = pre
            put_wide(nn(both(turned.at[0], p), pre), p)

        over_groups(body, before=arrival(GM2, m))
        exchange(GM1, m)

    def input_adjoint(m):
        def body(p):
            weight = jnp.concatenate([weights[RF, p], weights[RF, p + half]], 1)
            grad = tn(recv[GM1, m, p], weight)
            for q in (0, 1):
                at = lanes(p + q * half)
                part = grad[q * MIC : (q + 1) * MIC, q * BLK : (q + 1) * BLK]
                adj[rows(m), at] = (ups[rows(m), at].astype(F32) + part).astype(BF)

        def after(g):
            @pl.when(jnp.logical_not(is_first))
            def _():
                for q in (0, 1):
                    part = passed(m, g, q)
                    pltpu.make_async_remote_copy(
                        src_ref=adj.at[part],
                        dst_ref=ups.at[part],
                        send_sem=p_send.at[m, g, q],
                        recv_sem=p_recv.at[m, g, q],
                        device_id={"section": below},
                        device_id_type=MESH,
                    ).start()

        over_groups(body, before=arrival(GM1, m), after=after)

    def wide_gradients(m):
        def body(p):
            for f, left, right in (
                (RS, recv[GM2, m, p], act[m, p]),
                (LF, gpre[m, p], recv[FM, m, p]),
            ):
                grad = nt(masked(left), right)
                sums[f, p] += grad[:BLK]
                sums[f, p + half] += grad[BLK:]

        over_groups(body)

    def narrow_gradient(f, m, p, left, ref):
        grad = nn(left, diagonal(ref, m, p))
        sums[f, p] += grad[:, :BLK]
        sums[f, p + half] += grad[:, BLK:]

    def gradient_rf(m):
        over_groups(lambda p: narrow_gradient(RF, m, p, recv[GM1, m, p], x))

    def gradient_ls(m):
        over_groups(
            lambda p: narrow_gradient(LS, m, p, recv[SM, m, p], ups), before=arrival(SM, m)
        )

    def turn(p):
        for b in (p, p + half):
            turned[0, b] = weights[LF, b].astype(F32).T.astype(BF)
            turned[1, b] = weights[RS, b].astype(F32).T.astype(BF)

    steps = Z // 2

    def advance(*items):
        for f, k in items:
            if k < steps:
                gather_step(f, k)
            else:
                gather_end(f)

    for k in range(steps):
        advance((RF, k), (LS, k))
    advance((LF, 0), (RS, 0), (RF, steps), (LS, steps))

    def repeat(first, end, body):
        def step(m, carry):
            body(m)
            return carry

        lax.fori_loop(first, end, step, 0)

    def chain_of_last():
        def feed(m):
            first_mid(m)
            grad_mid_second(m, False)

        def pull(m):
            activations(m)
            grad_mid_first(m)

        top_copy.wait()
        feed(0)
        advance((LF, 1), (RS, 1))
        feed(1)
        advance((LF, 2), (RS, 2), (LF, 3), (RS, 3), (LF, 4), (RS, 4))
        over_groups(turn)
        def steady(m):
            pull(m)
            feed(m + 2)
            input_adjoint(m)

        def ending(m):
            pull(m)
            input_adjoint(m)

        repeat(0, M - 2, steady)
        repeat(M - 2, M, ending)
        repeat(0, M, second_mid)

        def own_gradients(m):
            wide_gradients(m)
            gradient_rf(m)

        repeat(0, M, own_gradients)
        repeat(0, M, gradient_ls)
        for f, k in ((LS, 0), (RS, 0), (LF, 0), (LS, 1), (LS, 2), (LS, 3)):
            scatter_step(f, k)

    def chain_of_others():
        for k in range(1, steps):
            first_mid(k - 1)
            advance((LF, k), (RS, k))
        repeat(steps - 1, M, first_mid)
        advance((LF, steps), (RS, steps))

        def forward(m):
            activations(m)
            pl.when(early)(lambda: second_mid(m))

        repeat(0, M, forward)
        over_groups(turn)

        def steady(m):
            grad_mid_first(m)
            grad_mid_second(m + 1, True)
            wide_gradients(m)
            pl.when(early)(lambda: gradient_ls(m + 1))
            input_adjoint(m)
            gradient_rf(m)

        grad_mid_second(0, True)
        pl.when(early)(lambda: gradient_ls(0))
        repeat(0, M - 2, steady)
        m = M - 2
        grad_mid_first(m)
        grad_mid_second(m + 1, True)
        pl.when(early)(lambda: gradient_ls(M - 1))
        pl.when(early)(lambda: scatter_step(LS, 0))
        wide_gradients(m)
        input_adjoint(m)
        pl.when(early)(lambda: scatter_step(LS, 1))
        gradient_rf(m)
        m = M - 1
        grad_mid_first(m)
        pl.when(early)(lambda: scatter_step(LS, 2))
        wide_gradients(m)
        scatter_step(RS, 0)
        scatter_step(LF, 0)
        pl.when(early)(lambda: scatter_step(LS, 3))
        input_adjoint(m)
        gradient_rf(m)

        @pl.when(jnp.logical_not(early))
        def _():
            repeat(0, M, second_mid)
            repeat(0, M, gradient_ls)
            for k in range(steps):
                scatter_step(LS, k)

    pl.when(is_last)(chain_of_last)
    pl.when(jnp.logical_not(is_last))(chain_of_others)

    scatter_step(RF, 0)
    for k in range(1, steps):
        for f in (RS, LF, RF):
            scatter_step(f, k)
    collect(LS, True)
    collect(RS)
    collect(LF)
    collect(RF)

    for f in range(4):
        wait(weights.at[f, pl.ds(0, (Z - 1) * SH)], w_send.at[f])
        wait(weights.at[f, pl.ds(0, (Z - 1) * SH)], r_send.at[f])
    for p in range(4):
        for m in range(M):
            wait(send.at[p, m, pl.ds(0, H - 1)], a_send.at[p, m])

    @pl.when(jnp.logical_not(is_first))
    def _():
        for m in range(M):
            for g in range(groups):
                for q in (0, 1):
                    wait(adj.at[passed(m, g, q)], p_send.at[m, g, q])


def solution(mesh):
    S, H, Z = (mesh.shape[name] for name in ("section", "hidden", "tok"))

    def on_device(section_inputs, top_adjoint, right_first, left_first, right_second, left_second):
        tokens, width = top_adjoint.shape
        M, NB, SH = tokens // MIC, width // BLK, right_first.shape[1]
        half = NB // 2
        groups = half // GRP
        scale = 1.0 / math.sqrt(tokens * Z)
        vmem = pl.BlockSpec(memory_space=pltpu.VMEM)
        dma = pltpu.SemaphoreType.DMA
        adjoint, grads = pl.pallas_call(
            functools.partial(kernel, S, H, Z, scale),
            out_shape=[
                jax.ShapeDtypeStruct((tokens, width), BF),
                jax.ShapeDtypeStruct((4, SH, BLK, BLK), F32),
            ],
            in_specs=[vmem, pl.BlockSpec(memory_space=pl.ANY)] + [vmem] * 4,
            out_specs=[vmem] * 2,
            scratch_shapes=[
                pltpu.VMEM((tokens, width), BF),
                pltpu.VMEM((4, M, H, half, NB, LANES), BF),
                pltpu.VMEM((4, M, half, BLK, LANES), BF),
                pltpu.VMEM((M, half, BLK, LANES), BF),
                pltpu.VMEM((M, half, BLK, LANES), F32),
                pltpu.VMEM((M, half, BLK, LANES), BF),
                pltpu.VMEM((H * half * NB, LANES), F32),
                pltpu.VMEM((4, NB, BLK, BLK), BF),
                pltpu.VMEM((2, NB, BLK, BLK), BF),
                pltpu.VMEM((4, NB, BLK, BLK), F32),
                pltpu.VMEM((4, 2, Z // 2, SH, BLK, BLK), BF),
                pltpu.VMEM((4, 2, Z // 2, SH, BLK, BLK), BF),
                dma,
                dma((4,)),
                dma((4, 2, Z // 2)),
                dma((4, M)),
                dma((4, M, groups)),
                dma((M, groups, 2)),
                dma((M, groups, 2)),
                dma((4,)),
                dma((4, 2, Z // 2)),
            ],
            compiler_params=pltpu.CompilerParams(
                collective_id=0, has_side_effects=True, vmem_limit_bytes=56 * 1024 * 1024
            ),
        )(section_inputs[0], top_adjoint, right_first[0], left_first[0], right_second[0], left_second[0])
        return adjoint[None], *(grads[f][None] for f in (RF, LF, RS, LS))

    act = P("section", "tok", "hidden")
    weight = P("section", ("hidden", "tok"), None, None)
    return jax.shard_map(
        on_device,
        mesh=mesh,
        in_specs=(act, P("tok", "hidden"), weight, weight, weight, weight),
        out_specs=(act, weight, weight, weight, weight),
        check_vma=False,
    )
```

time: 197 us -> 169 us (0.86)
  Pallas kernels: 190 us -> 163 us
    pallas_call x1, Pallas kernels: 190 us -> 163 us  [on_device(): pl.pallas_call(functools.partial(kernel, S, H, Z, scale), out_shape=[jax....]
    unnamed x13 -> x1, local copies, waits for them, and re-layouts: 5.42 us -> 2.73 us
where the time goes in v4:
time: 169 us
  Pallas kernels  163 us (96%)
  local copies, waits for them, and re-layouts  4.62 us (3%)
    pallas_call x1, Pallas kernels, on_device(): pl.pallas_call(functools.partial(kernel, S, H, Z, scale), out_shape=[jax....  163 us

profile of v4, /device:TPU:1, one launch (start us, length us, event | category | flops | bytes accessed | tf_op | source)
XLA Modules:
  0.0 168.5 jit_solution(15740507729388950982)
XLA Ops:
  0.6 163.3 %shard_map.101 = (bf16[384,2048]{1,0:T(8,128)(2,1)}, f32[4,2,128,128]{3,2,1,0:T(8,128)}) custom-call(bf16[384,2048]{1,0:T(8,128)(2,1)} %bitcast.7, bf16[384,2048]{1,0:T(8,128)(2,1)} %top.1, bf16[2,128,128]{2,1,0:T(8,128)(2,1)} %bitcast.8, bf16[2,128,128]{2,1,0:T(8,128)(2,1)} %bitcast.9, bf16[2,128,128]{2,1,0:T(8,128)(2,1)} %bitcast.10, ...), custom_call_target="tpu_custom_call" | custom-call | tf_op jit(solution)/shard_map/pallas_call | solution.py:487
  163.9 1.9 %fusion = (f32[1,2,128,128]{3,2,1,0:T(8,128)}, f32[1,2,128,128]{3,2,1,0:T(8,128)}, f32[1,2,128,128]{3,2,1,0:T(8,128)}, f32[1,2,128,128]{3,2,1,0:T(8,128)}) fusion(f32[4,2,128,128]{3,2,1,0:T(8,128)} %get-tuple-element.8), kind=kLoop, calls=%fused_computation | loop fusion | bytes 1048576 | tf_op jit(solution)/shard_map/slice | solution.py:522
  165.8 2.7 %copy.12 = bf16[1,384,2048]{2,1,0:T(8,128)(2,1)} copy(bf16[1,384,2048]{2,1,0:T(8,128)(2,1)} %bitcast.6) | data formatting | bytes 3145728

commit v5 on v4

--- a/solution.py
+++ b/solution.py
@@ -46,9 +46,9 @@
 
 def kernel(
     S, H, Z, scale,
-    x, top, rf, lf, rs, ls,
-    adj, grads,
-    ups, send, recv, act, der, gpre, stage, weights, turned, sums, part_send, part_recv,
+    x_in, top, rf, lf, rs, ls,
+    adj_out, grads,
+    x, adj, x_sem, o_sem, ups, send, recv, act, der, gpre, stage, weights, turned, sums, part_send, part_recv,
     top_sem, w_send, w_recv, a_send, a_recv, p_send, p_recv, r_send, r_recv,
 ):
     sec, h, z = (lax.axis_index(name) for name in ("section", "hidden", "tok"))
@@ -67,6 +67,8 @@
     def wait(view, sem):
         pltpu.make_async_copy(view, view, sem).wait()
 
+    x_copy = pltpu.make_async_copy(x_in, x, x_sem)
+    x_copy.start()
     top_copy = pltpu.make_async_copy(top, ups, top_sem)
 
     @pl.when(is_last)
@@ -307,6 +309,7 @@
                     ).start()
 
         over_groups(body, before=arrival(GM1, m), after=after)
+        pltpu.make_async_copy(adj.at[rows(m)], adj_out.at[rows(m)], o_sem.at[m]).start()
 
     def wide_gradients(m):
         def body(p):
@@ -363,27 +366,26 @@
             first_mid(m)
             grad_mid_second(m, False)
 
-        def pull(m):
-            activations(m)
-            grad_mid_first(m)
-
         top_copy.wait()
         feed(0)
         advance((LF, 1), (RS, 1))
         feed(1)
         advance((LF, 2), (RS, 2), (LF, 3), (RS, 3), (LF, 4), (RS, 4))
         over_groups(turn)
+        activations(0)
+
         def steady(m):
-            pull(m)
+            grad_mid_first(m)
             feed(m + 2)
+            activations(m + 1)
             input_adjoint(m)
 
-        def ending(m):
-            pull(m)
-            input_adjoint(m)
-
         repeat(0, M - 2, steady)
-        repeat(M - 2, M, ending)
+        grad_mid_first(M - 2)
+        activations(M - 1)
+        input_adjoint(M - 2)
+        grad_mid_first(M - 1)
+        input_adjoint(M - 1)
         repeat(0, M, second_mid)
 
         def own_gradients(m):
@@ -411,8 +413,8 @@
 
         def steady(m):
             grad_mid_first(m)
+            wide_gradients(m)
             grad_mid_second(m + 1, True)
-            wide_gradients(m)
             pl.when(early)(lambda: gradient_ls(m + 1))
             input_adjoint(m)
             gradient_rf(m)
@@ -446,6 +448,7 @@
             for k in range(steps):
                 scatter_step(LS, k)
 
+    x_copy.wait()
     pl.when(is_last)(chain_of_last)
     pl.when(jnp.logical_not(is_last))(chain_of_others)
 
@@ -458,6 +461,8 @@
     collect(LF)
     collect(RF)
 
+    for m in range(M):
+        pltpu.make_async_copy(adj.at[rows(m)], adj_out.at[rows(m)], o_sem.at[m]).wait()
     for f in range(4):
         wait(weights.at[f, pl.ds(0, (Z - 1) * SH)], w_send.at[f])
         wait(weights.at[f, pl.ds(0, (Z - 1) * SH)], r_send.at[f])
@@ -490,9 +495,13 @@
                 jax.ShapeDtypeStruct((tokens, width), BF),
                 jax.ShapeDtypeStruct((4, SH, BLK, BLK), F32),
             ],
-            in_specs=[vmem, pl.BlockSpec(memory_space=pl.ANY)] + [vmem] * 4,
-            out_specs=[vmem] * 2,
+            in_specs=[pl.BlockSpec(memory_space=pl.ANY)] * 2 + [vmem] * 4,
+            out_specs=[pl.BlockSpec(memory_space=pl.ANY), vmem],
             scratch_shapes=[
+                pltpu.VMEM((tokens, width), BF),
+                pltpu.VMEM((tokens, width), BF),
+                dma,
+                dma((M,)),
                 pltpu.VMEM((tokens, width), BF),
                 pltpu.VMEM((4, M, H, half, NB, LANES), BF),
                 pltpu.VMEM((4, M, half, BLK, LANES), BF),

time: 169 us -> 169 us (level)
  no operation moved by 1% of the time
where the time goes in v5:
time: 169 us
  Pallas kernels  163 us (96%)
  local copies, waits for them, and re-layouts  4.62 us (3%)
    pallas_call x1, Pallas kernels, on_device(): pl.pallas_call(functools.partial(kernel, S, H, Z, scale), out_shape=[jax....  163 us

profile of v5, /device:TPU:1, one launch (start us, length us, event | category | flops | bytes accessed | tf_op | source)
XLA Modules:
  0.0 168.7 jit_solution(5365139358470484624)
XLA Ops:
  0.6 163.4 %shard_map.101 = (bf16[384,2048]{1,0:T(8,128)(2,1)}, f32[4,2,128,128]{3,2,1,0:T(8,128)}) custom-call(bf16[384,2048]{1,0:T(8,128)(2,1)} %bitcast.7, bf16[384,2048]{1,0:T(8,128)(2,1)} %top.1, bf16[2,128,128]{2,1,0:T(8,128)(2,1)} %bitcast.8, bf16[2,128,128]{2,1,0:T(8,128)(2,1)} %bitcast.9, bf16[2,128,128]{2,1,0:T(8,128)(2,1)} %bitcast.10, ...), custom_call_target="tpu_custom_call" | custom-call | tf_op jit(solution)/shard_map/pallas_call | solution.py:492
  164.1 1.9 %fusion = (f32[1,2,128,128]{3,2,1,0:T(8,128)}, f32[1,2,128,128]{3,2,1,0:T(8,128)}, f32[1,2,128,128]{3,2,1,0:T(8,128)}, f32[1,2,128,128]{3,2,1,0:T(8,128)}) fusion(f32[4,2,128,128]{3,2,1,0:T(8,128)} %get-tuple-element.8), kind=kLoop, calls=%fused_computation | loop fusion | bytes 1048576 | tf_op jit(solution)/shard_map/slice | solution.py:531
  166.0 2.7 %copy.12 = bf16[1,384,2048]{2,1,0:T(8,128)(2,1)} copy(bf16[1,384,2048]{2,1,0:T(8,128)(2,1)} %bitcast.6) | data formatting | bytes 3145728

commit v6 on v5

--- a/solution.py
+++ b/solution.py
@@ -111,47 +111,50 @@
     def gather_step(f, k):
         for way in (0, 1):
             if k < hops(f, way):
-                part = weights.at[f, share(ahead(1 - way, k) if k else z)]
-                if k:
-                    wait(part, w_recv.at[f, way, k - 1])
-                pltpu.make_async_remote_copy(
-                    src_ref=part,
-                    dst_ref=part,
-                    send_sem=w_send.at[f],
-                    recv_sem=w_recv.at[f, way, k],
-                    device_id=next_on(way),
-                    device_id_type=MESH,
-                ).start()
+                origin = ahead(1 - way, k) if k else z
+                for s in range(SH):
+                    part = weights.at[f, origin * SH + s]
+                    if k:
+                        wait(part, w_recv.at[f, way, k - 1, s])
+                    pltpu.make_async_remote_copy(
+                        src_ref=part,
+                        dst_ref=part,
+                        send_sem=w_send.at[f],
+                        recv_sem=w_recv.at[f, way, k, s],
+                        device_id=next_on(way),
+                        device_id_type=MESH,
+                    ).start()
 
     def gather_end(f):
         for way in (0, 1):
-            wait(weights.at[f, share(0)], w_recv.at[f, way, hops(f, way) - 1])
+            for s in range(SH):
+                wait(weights.at[f, s], w_recv.at[f, way, hops(f, way) - 1, s])
 
     def scatter_step(f, k):
         for way in (0, 1):
             n = hops(f, way)
             if k < n:
                 target = ahead(way, n - k)
-                if k:
-                    wait(part_recv.at[f, way, k - 1], r_recv.at[f, way, k - 1])
                 for s in range(SH):
                     total = sums[f, target * SH + s]
                     if k:
+                        wait(part_recv.at[f, way, k - 1, s], r_recv.at[f, way, k - 1, s])
                         total = total + part_recv[f, way, k - 1, s].astype(F32)
                     part_send[f, way, k, s] = total.astype(BF)
-                pltpu.make_async_remote_copy(
-                    src_ref=part_send.at[f, way, k],
-                    dst_ref=part_recv.at[f, way, k],
-                    send_sem=r_send.at[f],
-                    recv_sem=r_recv.at[f, way, k],
-                    device_id=next_on(way),
-                    device_id_type=MESH,
-                ).start()
+                    pltpu.make_async_remote_copy(
+                        src_ref=part_send.at[f, way, k, s],
+                        dst_ref=part_recv.at[f, way, k, s],
+                        send_sem=r_send.at[f],
+                        recv_sem=r_recv.at[f, way, k, s],
+                        device_id=next_on(way),
+                        device_id_type=MESH,
+                    ).start()
 
     def collect(f, turn=False):
         for way in (0, 1):
             last = hops(f, way) - 1
-            wait(part_recv.at[f, way, last], r_recv.at[f, way, last])
+            for s in range(SH):
+                wait(part_recv.at[f, way, last, s], r_recv.at[f, way, last, s])
         for s in range(SH):
             total = sums[f, z * SH + s]
             for way in (0, 1):
@@ -516,13 +519,13 @@
                 pltpu.VMEM((4, 2, Z // 2, SH, BLK, BLK), BF),
                 dma,
                 dma((4,)),
-                dma((4, 2, Z // 2)),
+                dma((4, 2, Z // 2, SH)),
                 dma((4, M)),
                 dma((4, M, groups)),
                 dma((M, groups, 2)),
                 dma((M, groups, 2)),
                 dma((4,)),
-                dma((4, 2, Z // 2)),
+                dma((4, 2, Z // 2, SH)),
             ],
             compiler_params=pltpu.CompilerParams(
                 collective_id=0, has_side_effects=True, vmem_limit_bytes=56 * 1024 * 1024

time: 169 us -> 168 us (level)
  no operation moved by 1% of the time
where the time goes in v6:
time: 168 us; the launch traced here: 167 us
  Pallas kernels  162 us (96%)
  local copies, waits for them, and re-layouts  4.62 us (3%)
    pallas_call x1, Pallas kernels, on_device(): pl.pallas_call(functools.partial(kernel, S, H, Z, scale), out_shape=[jax....  162 us

profile of v6, /device:TPU:1, one launch (start us, length us, event | category | flops | bytes accessed | tf_op | source)
XLA Modules:
  0.0 167.3 jit_solution(12477395403973561565)
XLA Ops:
  0.6 162.1 %shard_map.101 = (bf16[384,2048]{1,0:T(8,128)(2,1)}, f32[4,2,128,128]{3,2,1,0:T(8,128)}) custom-call(bf16[384,2048]{1,0:T(8,128)(2,1)} %bitcast.7, bf16[384,2048]{1,0:T(8,128)(2,1)} %top.1, bf16[2,128,128]{2,1,0:T(8,128)(2,1)} %bitcast.8, bf16[2,128,128]{2,1,0:T(8,128)(2,1)} %bitcast.9, bf16[2,128,128]{2,1,0:T(8,128)(2,1)} %bitcast.10, ...), custom_call_target="tpu_custom_call" | custom-call | tf_op jit(solution)/shard_map/pallas_call | solution.py:495
  162.7 1.9 %fusion = (f32[1,2,128,128]{3,2,1,0:T(8,128)}, f32[1,2,128,128]{3,2,1,0:T(8,128)}, f32[1,2,128,128]{3,2,1,0:T(8,128)}, f32[1,2,128,128]{3,2,1,0:T(8,128)}) fusion(f32[4,2,128,128]{3,2,1,0:T(8,128)} %get-tuple-element.8), kind=kLoop, calls=%fused_computation | loop fusion | bytes 1048576 | tf_op jit(solution)/shard_map/slice | solution.py:534
  164.6 2.7 %copy.12 = bf16[1,384,2048]{2,1,0:T(8,128)(2,1)} copy(bf16[1,384,2048]{2,1,0:T(8,128)(2,1)} %bitcast.6) | data formatting | bytes 3145728
